TPU v7x, 32 devices: a whole 2x2x4 slice. The times are simulated.
32 devices in a mesh: grp: 1, dev: 16 (over z, y, core), section: 2 (over x), tp: 1.
Axes of the slice: x: 2, y: 2, z: 4, core: 2. Of those that a mesh axis runs over, the one named last changes fastest.
Arguments:
- prompt_pages: bfloat16 [32, 32, 16, 576], P(('grp', 'dev', 'section', 'tp')), may hold values from -6 to 6
- send_page: int32 [32, 32], P(('grp', 'dev', 'section', 'tp')), may hold values from -1 to 31, as said below
- page_table: int32 [32, 2, 16], P(('grp', 'dev', 'section', 'tp')), may hold values from -1 to 31, as said below
- context_len: int32 [32, 2], P(('grp', 'dev', 'section', 'tp')), may hold values from 1 to 256, as said below
- new_latent: bfloat16 [32, 2, 4, 576], P(('grp', 'dev', 'section', 'tp')), may hold values from -8 to 8
- queries: bfloat16 [32, 2, 4, 64, 576], P(('grp', 'dev', 'section', 'tp')), may hold values from -120 to 120
- moe_rows: bfloat16 [32, 4, 3584], P(('grp', 'dev', 'section', 'tp')), may hold values from -6 to 6
- routing: int32 [32, 4, 8], P(('grp', 'dev', 'section', 'tp')), may hold values from 0 to 15, all different within a row; in each aligned block of 4 rows (0 to 3, 4 to 7, ..., all dimensions but the last counted through in order) at most 3 rows name the same one
- gate_weights: float32 [32, 4, 8], P(('grp', 'dev', 'section', 'tp')), may hold values from 0.05 to 0.5
- expert_gate: bfloat16 [16, 3584, 1024], P('dev', None, ('section', 'tp')), may hold values from -0.09375 to 0.09375
- expert_up: bfloat16 [16, 3584, 1024], P('dev', None, ('section', 'tp')), may hold values from -0.09375 to 0.09375
- expert_down: bfloat16 [16, 1024, 3584], P('dev', ('section', 'tp')), may hold values from -0.1875 to 0.1875
Outputs:
- attended: bfloat16 [32, 2, 4, 64, 512], P(('grp', 'dev', 'section', 'tp'))
- expert_out: bfloat16 [32, 4, 3584], P(('grp', 'dev', 'section', 'tp'))
Inputs may be any that keep to these rules, and one draw needn't show every extreme that they name: context_len of some request of every rank is exactly 256. `page_table`: of a rank's entries, those with p < ceil(context_len / 16) are distinct slots, all others -1. `send_page`: an outgoing slot holds a page exactly when the receiving rank's page_table names it; the pages of one rank named are distinct. `routing`: no rank names one expert in more than 3 of its assignments.
All inputs are finite; a program needn't handle non-finite values.
Results may differ from a plain program's by a relative error of at most 0.02.
Values may be sent and summed in bfloat16 or wider, within the bound.
No kernel may reach another device: no remote copies, remote signals or barrier semaphores. Data moves between devices by JAX's collectives and lax.ppermute only.
A program may use at most 64 MiB of HBM per device.

v0:
```python
import jax
import jax.numpy as jnp
from jax import lax
from jax.experimental import pallas as pl
from jax.experimental.pallas import tpu as pltpu
from jax.sharding import PartitionSpec as P

VDIM = 512
SCALE = 192.0 ** (-0.5)
RANK = ("dev", "section", "tp")
VMEM_LIMIT = 50 * 1024 * 1024


def levels_of(peers, blocks):
    low = blocks.bit_length() - 1
    bits = peers.bit_length() - 1
    far = [low + bit for bit in range(2, bits)]
    near = list(range(low)) + [low + bit for bit in range(1, min(bits, 2))]
    last = [low + bit for bit in range(min(bits, 1))]
    return far, near, last


def masks_of(bits):
    masks = [0]
    for bit in bits:
        masks += [mask | (1 << bit) for mask in masks]
    return masks


def exchange(value, mask):
    count = lax.axis_size(RANK)
    return lax.ppermute(value, RANK, [(at, at ^ mask) for at in range(count)])


def pairs_of(bits):
    return [bits[at : at + 2] for at in range(0, len(bits), 2)]


def collect(value, bits):
    masks = masks_of(bits)
    count = value.shape[0] // len(masks)
    total = value[:count].astype(jnp.float32)
    for turn in range(1, len(masks)):
        sent = value[turn * count : (turn + 1) * count]
        total = total + exchange(sent, masks[turn]).astype(jnp.float32)
    return total.astype(jnp.bfloat16)


def experts_kernel(
    first_ref, own_ref, got_ref, gate_hbm, up_hbm, down_hbm, kept_ref, sent_ref,
    rows_ref, hidden_ref, gate_ref, up_ref, down_ref, in_sem, down_sem,
):
    count = own_ref.shape[0]
    owned, width, units = gate_hbm.shape
    experts = first_ref[1]
    step = min(units, 256)
    wide = 512 if width % 512 == 0 else 128
    turns, ends = units // step, width // wide

    def load_in(which, own, turn):
        source, target = ((gate_hbm, gate_ref), (up_hbm, up_ref))[which]
        part = (own, slice(None), pl.ds(turn * step, step))
        return pltpu.make_async_copy(source.at[part], target.at[part], in_sem.at[which, own, turn])

    def load_down(own, turn):
        part = (own, slice(None), pl.ds(turn * wide, wide))
        return pltpu.make_async_copy(down_hbm.at[part], down_ref.at[part], down_sem.at[own, turn])

    for own in range(owned):
        for turn in range(turns):
            load_in(0, own, turn).start()
            load_in(1, own, turn).start()
    for turn in range(ends):
        for own in range(owned):
            load_down(own, turn).start()
    rows_ref[:count] = own_ref[...]
    rows_ref[count:] = got_ref[...]
    extra = rows_ref[:, width:].astype(jnp.float32)
    lane = lax.broadcasted_iota(jnp.int32, extra.shape, 1)
    weights = []
    for own in range(owned):
        expert = first_ref[0] + own
        named = (lane == expert) | (lane == expert + experts)
        weights.append(jnp.sum(jnp.where(named, extra, 0.0), axis=1, keepdims=True))
        for turn in range(turns):
            part = pl.ds(turn * step, step)
            x = rows_ref[:, :width]
            load_in(0, own, turn).wait()
            gate = jnp.dot(x, gate_ref[own, :, part], preferred_element_type=jnp.float32)
            load_in(1, own, turn).wait()
            up = jnp.dot(x, up_ref[own, :, part], preferred_element_type=jnp.float32)
            hidden = gate / (1.0 + jnp.exp(-gate)) * up
            hidden_ref[own, :, part] = hidden.astype(jnp.bfloat16)
    for turn in range(ends):
        part = pl.ds(turn * wide, wide)
        total = None
        for own in range(owned):
            load_down(own, turn).wait()
            term = jnp.dot(
                hidden_ref[own], down_ref[own, :, part], preferred_element_type=jnp.float32
            ) * weights[own]
            total = term if total is None else total + term
        total = total.astype(jnp.bfloat16)
        kept_ref[:, part] = total[:count]
        sent_ref[:, part] = total[count:]


def experts_of(own, got, first, experts, expert_gate, expert_up, expert_down):
    count, packed = own.shape
    owned, width, units = expert_gate.shape
    scalars = jnp.stack([first, jnp.int32(experts)])
    vmem = pl.BlockSpec(memory_space=pltpu.VMEM)
    hbm = pl.BlockSpec(memory_space=pltpu.HBM)
    half = jax.ShapeDtypeStruct((count, width), jnp.bfloat16)
    step = min(units, 256)
    wide = 512 if width % 512 == 0 else 128
    return pl.pallas_call(
        experts_kernel,
        out_shape=(half, half),
        in_specs=[pl.BlockSpec(memory_space=pltpu.SMEM), vmem, vmem, hbm, hbm, hbm],
        out_specs=(vmem, vmem),
        scratch_shapes=[
            pltpu.VMEM((2 * count, packed), jnp.bfloat16),
            pltpu.VMEM((owned, 2 * count, units), jnp.bfloat16),
            pltpu.VMEM(expert_gate.shape, jnp.bfloat16),
            pltpu.VMEM(expert_up.shape, jnp.bfloat16),
            pltpu.VMEM(expert_down.shape, jnp.bfloat16),
            pltpu.SemaphoreType.DMA((2, owned, units // step)),
            pltpu.SemaphoreType.DMA((owned, width // wide)),
        ],
        compiler_params=pltpu.CompilerParams(vmem_limit_bytes=VMEM_LIMIT),
        cost_estimate=pl.CostEstimate(
            flops=48 * count * owned * width * units,
            bytes_accessed=6 * owned * width * units,
            transcendentals=2 * count * owned * units,
        ),
        name="experts",
    )(scalars, own, got, expert_gate, expert_up, expert_down)


def attend(queries, new_latent, cache, lengths):
    steps = queries.shape[1]
    ctx = cache.shape[1]
    keys = jnp.concatenate([cache, new_latent], axis=1)
    scores = jnp.einsum("rshl,rkl->rshk", queries, keys, preferred_element_type=jnp.float32) * SCALE
    position = jnp.arange(ctx + steps)
    step_index = jnp.arange(steps)
    in_cache = position[None, :] < lengths[:, None]
    in_new = (position[None, :] >= ctx) & (position[None, :] - ctx <= step_index[:, None])
    allowed = in_cache[:, None, :] | in_new[None, :, :]
    scores = jnp.where(allowed[:, :, None, :], scores, -jnp.inf)
    top = jnp.max(scores, axis=-1, keepdims=True)
    weights = jnp.exp(scores - top)
    weights = (weights / jnp.sum(weights, axis=-1, keepdims=True)).astype(jnp.bfloat16)
    values = keys[:, :, :VDIM]
    return jnp.einsum("rshk,rkv->rshv", weights, values, preferred_element_type=jnp.float32).astype(
        jnp.bfloat16
    )


def body(
    prompt_pages,
    send_page,
    page_table,
    context_len,
    new_latent,
    queries,
    moe_rows,
    routing,
    gate_weights,
    expert_gate,
    expert_up,
    expert_down,
):
    peers = lax.axis_size("dev")
    pages = prompt_pages[0]
    outgoing_slots = send_page[0]
    page_len, width_lat = (pages.shape[1], pages.shape[2])
    capp = outgoing_slots.shape[0] // peers
    picked_pages = pages[jnp.maximum(outgoing_slots, 0)]
    owned = expert_gate.shape[0]
    experts = peers * owned
    rows = routing.shape[1]
    width = moe_rows.shape[2]
    named = routing[0][:, :, None] == jnp.arange(experts)[None, None, :]
    dense = jnp.sum(jnp.where(named, gate_weights[0][:, :, None], 0.0), axis=1)
    high = dense.astype(jnp.bfloat16)
    low = (dense - high.astype(jnp.float32)).astype(jnp.bfloat16)
    extra = jnp.concatenate([high, low], axis=1)
    pad = -extra.shape[1] % 128
    packed = jnp.concatenate([moe_rows[0], jnp.pad(extra, ((0, 0), (0, pad)))], axis=1)
    far, near, last = levels_of(peers, lax.axis_size(("section", "tp")))
    pooled = packed[None]
    for bits in pairs_of(far):
        pooled = jnp.concatenate([pooled] + [exchange(pooled, mask) for mask in masks_of(bits)[1:]], axis=0)
    pooled = lax.optimization_barrier(pooled).reshape(-1, packed.shape[1])
    pooled, picked_pages = lax.optimization_barrier((pooled, picked_pages))
    pooled = jnp.concatenate([pooled] + [exchange(pooled, mask) for mask in masks_of(near)[1:]], axis=0)
    arrived = lax.all_to_all(
        picked_pages.reshape(peers, capp, page_len, width_lat),
        "dev",
        split_axis=0,
        concat_axis=0,
        tiled=True,
    )
    arrived = arrived.reshape(peers * capp, page_len, width_lat)
    pooled = lax.optimization_barrier(pooled)
    other = masks_of(last)[-1]
    first = lax.axis_index("dev") * owned
    kept, sent = experts_of(
        pooled, exchange(pooled, other), first, experts, expert_gate, expert_up, expert_down
    )
    mixed = kept.astype(jnp.float32) + exchange(sent, other).astype(jnp.float32)
    mixed, arrived = lax.optimization_barrier((mixed.astype(jnp.bfloat16), arrived))
    for bits in [near] + pairs_of(far)[::-1]:
        mixed = collect(mixed, bits)

    table = page_table[0]
    requests, most_pages = table.shape
    cache = arrived[jnp.maximum(table, 0)].reshape(requests, most_pages * page_len, width_lat)
    attended = attend(queries[0], new_latent[0], cache, context_len[0])
    return (attended[None], mixed[None])


def solution(mesh):
    rank = ("grp",) + RANK
    return jax.shard_map(
        body,
        mesh=mesh,
        in_specs=(
            P(rank, None, None, None),
            P(rank, None),
            P(rank, None, None),
            P(rank, None),
            P(rank, None, None, None),
            P(rank, None, None, None, None),
            P(rank, None, None),
            P(rank, None, None),
            P(rank, None, None),
            P("dev", None, ("section", "tp")),
            P("dev", None, ("section", "tp")),
            P("dev", ("section", "tp"), None),
        ),
        out_specs=(
            P(rank, None, None, None, None),
            P(rank, None, None),
        ),
        check_vma=False,
    )
```

profile of v0, /device:TPU:0, one launch (start us, length us, event | category | flops | bytes accessed | tf_op | source)
XLA Modules:
  0.0 70.3 jit_solution(1898139082546558792)
XLA Ops:
  0.7 0.8 %select_reduce_fusion = f32[4,16]{1,0:T(4,128)S(1)} fusion(f32[4,8]{1,0:T(4,128)} %bitcast.54, s32[4,8]{1,0:T(4,128)} %bitcast.55), kind=kLoop, calls=%fused_computation.27 | loop fusion | flops 1472 | bytes 512 | tf_op jit(solution)/shard_map/reduce_sum | solution.py:186
  1.6 0.8 %maximum_bitcast_fusion = bf16[1,4,3712]{2,1,0:T(4,128)(2,1)S(1)} fusion(bf16[4,128]{1,0:T(4,128)(2,1)S(1)} %fusion.22, bf16[4,3584]{1,0:T(4,128)(2,1)} %bitcast.53), kind=kLoop, calls=%fused_computation.25 | loop fusion | flops 59392 | bytes 59392 | tf_op jit(solution)/shard_map/broadcast_in_dim | solution.py:193
  2.4 3.1 %collective-permute-start = (bf16[1,4,3712]{2,1,0:T(4,128)(2,1)S(1)}, bf16[1,4,3712]{2,1,0:T(4,128)(2,1)S(1)}, u32[]{:S(2)}, u32[]{:S(2)}) collective-permute-start(bf16[1,4,3712]{2,1,0:T(4,128)(2,1)S(1)} %maximum_bitcast_fusion), channel_id=1, source_target_pairs={{0,8},{1,9},{2,10},{3,11},{4,12},{5,13},{6,14},{7,15},{8,0},{9,1},... | collective-permute-start | bytes 89096 | tf_op jit(solution)/shard_map/ppermute | solution.py:32
  5.4 2.6 %collective-permute-start.1 = (bf16[1,4,3712]{2,1,0:T(4,128)(2,1)S(1)}, bf16[1,4,3712]{2,1,0:T(4,128)(2,1)S(1)}, u32[]{:S(2)}, u32[]{:S(2)}) collective-permute-start(bf16[1,4,3712]{2,1,0:T(4,128)(2,1)S(1)} %maximum_bitcast_fusion), channel_id=1, source_target_pairs={{0,16},{1,17},{2,18},{3,19},{4,20},{5,21},{6,22},{7,23},{8,24},{9,... | collective-permute-start | bytes 89096 | tf_op jit(solution)/shard_map/ppermute | solution.py:32
  8.0 0.7 maximum_bitcast_fusion.1
  8.7 1.5 %gather_fusion = bf16[32,16,576]{2,1,0:T(8,128)(2,1)} fusion(bf16[32,16,576]{2,1,0:T(8,128)(2,1)S(1)} %bitcast.48, s32[1024]{0:T(1024)S(1)} %pad_clamp_fusion.1), kind=kCustom, calls=%fused_computation | custom fusion | bytes 1179776 | tf_op jit(solution)/shard_map/gather | solution.py:180
  10.2 0.5 collective-permute-done.1
  10.7 3.0 %collective-permute-done.2 = bf16[1,4,3712]{2,1,0:T(4,128)(2,1)S(1)} collective-permute-done((bf16[1,4,3712]{2,1,0:T(4,128)(2,1)S(1)}, bf16[1,4,3712]{2,1,0:T(4,128)(2,1)S(1)}, u32[]{:S(2)}, u32[]{:S(2)}) %collective-permute-start.2) | collective-permute-done | bytes 29728 | tf_op jit(solution)/shard_map/ppermute | solution.py:32
  13.9 1.6 %collective-permute-start.3 = (bf16[16,3712]{1,0:T(8,128)(2,1)S(1)}, bf16[16,3712]{1,0:T(8,128)(2,1)S(1)}, u32[]{:S(2)}, u32[]{:S(2)}) collective-permute-start(bf16[16,3712]{1,0:T(8,128)(2,1)S(1)} %reshape.110), channel_id=1, source_target_pairs={{0,1},{1,0},{2,3},{3,2},{4,5},{5,4},{6,7},{7,6},{8,9},{9,8},{10,11... | collective-permute-start | bytes 356360 | tf_op jit(solution)/shard_map/ppermute | solution.py:32
  15.4 1.5 %collective-permute-start.4 = (bf16[16,3712]{1,0:T(8,128)(2,1)S(1)}, bf16[16,3712]{1,0:T(8,128)(2,1)S(1)}, u32[]{:S(2)}, u32[]{:S(2)}) collective-permute-start(bf16[16,3712]{1,0:T(8,128)(2,1)S(1)} %reshape.110), channel_id=1, source_target_pairs={{0,4},{1,5},{2,6},{3,7},{4,0},{5,1},{6,2},{7,3},{8,12},{9,13},{10,... | collective-permute-start | bytes 356360 | tf_op jit(solution)/shard_map/ppermute | solution.py:32
  16.9 0.5 collective-permute-start.5
  17.4 2.3 %collective-permute-done.3 = bf16[16,3712]{1,0:T(8,128)(2,1)S(1)} collective-permute-done((bf16[16,3712]{1,0:T(8,128)(2,1)S(1)}, bf16[16,3712]{1,0:T(8,128)(2,1)S(1)}, u32[]{:S(2)}, u32[]{:S(2)}) %collective-permute-start.3) | collective-permute-done | bytes 118816 | tf_op jit(solution)/shard_map/ppermute | solution.py:32
  19.7 1.3 %collective-permute-done.4 = bf16[16,3712]{1,0:T(8,128)(2,1)S(1)} collective-permute-done((bf16[16,3712]{1,0:T(8,128)(2,1)S(1)}, bf16[16,3712]{1,0:T(8,128)(2,1)S(1)}, u32[]{:S(2)}, u32[]{:S(2)}) %collective-permute-start.4) | collective-permute-done | bytes 118816 | tf_op jit(solution)/shard_map/ppermute | solution.py:32
  21.0 1.7 %collective-permute-done.5 = bf16[16,3712]{1,0:T(8,128)(2,1)S(1)} collective-permute-done((bf16[16,3712]{1,0:T(8,128)(2,1)S(1)}, bf16[16,3712]{1,0:T(8,128)(2,1)S(1)}, u32[]{:S(2)}, u32[]{:S(2)}) %collective-permute-start.5) | collective-permute-done | bytes 118816 | tf_op jit(solution)/shard_map/ppermute | solution.py:32
  23.0 1.6 %collective-permute-done.6.got_ref = bf16[64,3712]{1,0:T(8,128)(2,1)S(1)} collective-permute-done((bf16[64,3712]{1,0:T(8,128)(2,1)S(1)}, bf16[64,3712]{1,0:T(8,128)(2,1)S(1)}, u32[]{:S(2)}, u32[]{:S(2)}) %collective-permute-start.6) | collective-permute-done | bytes 475168 | tf_op jit(solution)/shard_map/ppermute | solution.py:32
  24.6 7.0 %experts.1 = (bf16[64,3584]{1,0:T(8,128)(2,1)S(1)}, bf16[64,3584]{1,0:T(8,128)(2,1)S(1)}) custom-call(s32[2]{0:T(128)S(1)} %pad_add_fusion.first_ref, bf16[64,3712]{1,0:T(8,128)(2,1)S(1)} %pad_maximum_fusion.1.own_ref, bf16[64,3712]{1,0:T(8,128)(2,1)S(1)} %collective-permute-done.6.got_ref, bf16[1,3584,512]{2,1,0:T(8,128)(2,1)} %gate_hbm.1, ...), custom_call_target="tpu_custom_call" | custom-call | flops 5637144576 | bytes 11010048 | tf_op jit(solution)/shard_map/experts/pallas_call | solution.py:117
  31.6 0.2 collective-permute-start.7
  31.9 3.6 %all-to-all-start = ((bf16[16,2,16,576]{3,2,1,0:T(8,128)(2,1)}), bf16[16,2,16,576]{3,2,1,0:T(8,128)(2,1)S(1)}, u32[]{:S(2)}, u32[]{:S(2)}) async-start(bf16[16,2,16,576]{3,2,1,0:T(8,128)(2,1)} %bitcast.8), calls=%async_computation | async-start | bytes 1310720 | tf_op jit(solution)/shard_map/all_to_all | solution.py:199
  35.6 16.4 %all-to-all-done = bf16[16,2,16,576]{3,2,1,0:T(8,128)(2,1)S(1)} async-done(((bf16[16,2,16,576]{3,2,1,0:T(8,128)(2,1)}), bf16[16,2,16,576]{3,2,1,0:T(8,128)(2,1)S(1)}, u32[]{:S(2)}, u32[]{:S(2)}) %all-to-all-start) | async-done | bytes 589856 | tf_op jit(solution)/shard_map/all_to_all | solution.py:199
  52.1 0.8 %collective-permute-start.10 = (bf16[16,3584]{1,0:T(8,128)(2,1)S(1)}, bf16[16,3584]{1,0:T(8,128)(2,1)S(1)}, u32[]{:S(2)}, u32[]{:S(2)}) collective-permute-start(bf16[16,3584]{1,0:T(8,128)(2,1)S(1)} %get-tuple-element.17), channel_id=1, source_target_pairs={{0,5},{1,4},{2,7},{3,6},{4,1},{5,0},{6,3},{7,2},{8,13},{9,12},{10,... | collective-permute-start | bytes 344072 | tf_op jit(solution)/shard_map/ppermute | solution.py:32
  52.8 1.5 %collective-permute-start.8 = (bf16[16,3584]{1,0:T(8,128)(2,1)S(1)}, bf16[16,3584]{1,0:T(8,128)(2,1)S(1)}, u32[]{:S(2)}, u32[]{:S(2)}) collective-permute-start(bf16[16,3584]{1,0:T(8,128)(2,1)S(1)} %get-tuple-element.16), channel_id=1, source_target_pairs={{0,1},{1,0},{2,3},{3,2},{4,5},{5,4},{6,7},{7,6},{8,9},{9,8},{10,11... | collective-permute-start | bytes 344072 | tf_op jit(solution)/shard_map/ppermute | solution.py:32
  54.3 1.3 %collective-permute-start.9 = (bf16[16,3584]{1,0:T(8,128)(2,1)S(1)}, bf16[16,3584]{1,0:T(8,128)(2,1)S(1)}, u32[]{:S(2)}, u32[]{:S(2)}) collective-permute-start(bf16[16,3584]{1,0:T(8,128)(2,1)S(1)} %get-tuple-element.18), channel_id=1, source_target_pairs={{0,4},{1,5},{2,6},{3,7},{4,0},{5,1},{6,2},{7,3},{8,12},{9,13},{10,... | collective-permute-start | bytes 344072 | tf_op jit(solution)/shard_map/ppermute | solution.py:32
  55.6 0.7 gather_fusion.1
  56.3 2.6 %fusion.4 = f32[2,4,64,260]{3,2,1,0:T(8,128)} fusion(bf16[2,4,576]{2,1,0:T(4,128)(2,1)S(1)} %bitcast.57, bf16[1,2,4,64,576]{4,3,2,1,0:T(8,128)(2,1)} %param.17, bf16[2,256,576]{2,1,0:T(8,128)(2,1)S(1)} %bitcast.50, pred[2,4,260]{2,1,0:T(4,128)(4,1)S(1)} %broadcast_or_fusion), kind=kOutput, calls=%fused_computation.8 | convolution fusion | flops 154818560 | bytes 1723424 | tf_op jit(solution)/shard_map/rshl,rkl->rshk/dot_general | solution.py:145
  58.9 0.7 %fusion.32 = f32[2,4,64]{2,1,0:T(4,128)S(1)} fusion(bf16[2,4,576]{2,1,0:T(4,128)(2,1)S(1)} %bitcast.58, bf16[1,2,4,64,576]{4,3,2,1,0:T(8,128)(2,1)S(1)} %copy-done.3, bf16[2,256,576]{2,1,0:T(8,128)(2,1)S(1)} %bitcast.51, pred[2,4,260]{2,1,0:T(4,128)(4,1)S(1)} %broadcast_or_fusion), kind=kOutput, calls=%fused_computation.53 | convolution fusion | flops 155085056 | bytes 1192992 | tf_op jit(solution)/shard_map/sub | solution.py:153
  59.7 0.9 %collective-permute-done.8 = bf16[16,3584]{1,0:T(8,128)(2,1)S(1)} collective-permute-done((bf16[16,3584]{1,0:T(8,128)(2,1)S(1)}, bf16[16,3584]{1,0:T(8,128)(2,1)S(1)}, u32[]{:S(2)}, u32[]{:S(2)}) %collective-permute-start.8) | collective-permute-done | bytes 114720 | tf_op jit(solution)/shard_map/ppermute | solution.py:32
  60.7 2.3 %collective-permute-start.11 = (bf16[4,3584]{1,0:T(4,128)(2,1)S(1)}, bf16[4,3584]{1,0:T(4,128)(2,1)S(1)}, u32[]{:S(2)}, u32[]{:S(2)}) collective-permute-start(bf16[4,3584]{1,0:T(4,128)(2,1)S(1)} %get-tuple-element.19), channel_id=1, source_target_pairs={{0,8},{1,9},{2,10},{3,11},{4,12},{5,13},{6,14},{7,15},{8,0},{9,1},... | collective-permute-start | bytes 86024 | tf_op jit(solution)/shard_map/ppermute | solution.py:32
  63.0 1.0 %collective-permute-start.12 = (bf16[4,3584]{1,0:T(4,128)(2,1)S(1)}, bf16[4,3584]{1,0:T(4,128)(2,1)S(1)}, u32[]{:S(2)}, u32[]{:S(2)}) collective-permute-start(bf16[4,3584]{1,0:T(4,128)(2,1)S(1)} %get-tuple-element.21), channel_id=1, source_target_pairs={{0,16},{1,17},{2,18},{3,19},{4,20},{5,21},{6,22},{7,23},{8,24},{9,... | collective-permute-start | bytes 86024 | tf_op jit(solution)/shard_map/ppermute | solution.py:32
  64.0 1.5 %collective-permute-start.13 = (bf16[4,3584]{1,0:T(4,128)(2,1)S(1)}, bf16[4,3584]{1,0:T(4,128)(2,1)S(1)}, u32[]{:S(2)}, u32[]{:S(2)}) collective-permute-start(bf16[4,3584]{1,0:T(4,128)(2,1)S(1)} %get-tuple-element.20), channel_id=1, source_target_pairs={{0,24},{1,25},{2,26},{3,27},{4,28},{5,29},{6,30},{7,31},{8,16},{9,... | collective-permute-start | bytes 86024 | tf_op jit(solution)/shard_map/ppermute | solution.py:32
  65.5 3.3 %fusion.5 = bf16[1,2,4,64,512]{4,3,2,1,0:T(8,128)(2,1)} fusion(bf16[2,256,576]{2,1,0:T(8,128)(2,1)S(1)} %bitcast.52, bf16[2,4,576]{2,1,0:T(4,128)(2,1)S(1)} %bitcast.59, f32[2,4,64]{2,1,0:T(4,128)S(1)} %fusion.32, f32[2,4,64,260]{3,2,1,0:T(8,128)} %fusion.4), kind=kOutput, calls=%fused_computation.9 | convolution fusion | flops 138042112 | bytes 2698240 | tf_op jit(solution)/shard_map/rshk,rkv->rshv/dot_general | solution.py:156
  68.8 0.9 %collective-permute-done.13 = bf16[4,3584]{1,0:T(4,128)(2,1)S(1)} collective-permute-done((bf16[4,3584]{1,0:T(4,128)(2,1)S(1)}, bf16[4,3584]{1,0:T(4,128)(2,1)S(1)}, u32[]{:S(2)}, u32[]{:S(2)}) %collective-permute-start.13) | collective-permute-done | bytes 28704 | tf_op jit(solution)/shard_map/ppermute | solution.py:32
  69.7 0.6 fusion.14
  (37 shorter events, 0.9 us)
Async XLA Ops:
  0.6 8.1 %copy-start = (bf16[1,32,16,576]{3,2,1,0:T(8,128)(2,1)S(1)}, bf16[1,32,16,576]{3,2,1,0:T(8,128)(2,1)}, u32[]{:S(2)}) copy-start(bf16[1,32,16,576]{3,2,1,0:T(8,128)(2,1)} %param.12) | copy-start | bytes 1769476
  0.6 16.8 %copy-start.1 = (s32[1,2,16]{2,1,0:T(2,128)S(1)}, s32[1,2,16]{2,1,0:T(2,128)}, u32[]{:S(2)}) copy-start(s32[1,2,16]{2,1,0:T(2,128)} %param.14) | copy-start | bytes 388
  2.4 7.8 %collective-permute-start = (bf16[1,4,3712]{2,1,0:T(4,128)(2,1)S(1)}, bf16[1,4,3712]{2,1,0:T(4,128)(2,1)S(1)}, u32[]{:S(2)}, u32[]{:S(2)}) collective-permute-start(bf16[1,4,3712]{2,1,0:T(4,128)(2,1)S(1)} %maximum_bitcast_fusion), channel_id=1, source_target_pairs={{0,8},{1,9},{2,10},{3,11},{4,12},{5,13},{6,14},{7,15},{8,0},{9,1},... | collective-permute-start | bytes 89096 | tf_op jit(solution)/shard_map/ppermute | solution.py:32
  5.4 5.3 %collective-permute-start.1 = (bf16[1,4,3712]{2,1,0:T(4,128)(2,1)S(1)}, bf16[1,4,3712]{2,1,0:T(4,128)(2,1)S(1)}, u32[]{:S(2)}, u32[]{:S(2)}) collective-permute-start(bf16[1,4,3712]{2,1,0:T(4,128)(2,1)S(1)} %maximum_bitcast_fusion), channel_id=1, source_target_pairs={{0,16},{1,17},{2,18},{3,19},{4,20},{5,21},{6,22},{7,23},{8,24},{9,... | collective-permute-start | bytes 89096 | tf_op jit(solution)/shard_map/ppermute | solution.py:32
  8.0 5.7 %collective-permute-start.2 = (bf16[1,4,3712]{2,1,0:T(4,128)(2,1)S(1)}, bf16[1,4,3712]{2,1,0:T(4,128)(2,1)S(1)}, u32[]{:S(2)}, u32[]{:S(2)}) collective-permute-start(bf16[1,4,3712]{2,1,0:T(4,128)(2,1)S(1)} %maximum_bitcast_fusion), channel_id=1, source_target_pairs={{0,24},{1,25},{2,26},{3,27},{4,28},{5,29},{6,30},{7,31},{8,16},{9,... | collective-permute-start | bytes 89096 | tf_op jit(solution)/shard_map/ppermute | solution.py:32
  8.7 14.3 %copy-start.2 = (s32[1,2]{1,0:T(1,128)S(1)}, s32[1,2]{1,0:T(1,128)}, u32[]{:S(2)}) copy-start(s32[1,2]{1,0:T(1,128)} %param.15) | copy-start | bytes 28
  13.9 5.8 %collective-permute-start.3 = (bf16[16,3712]{1,0:T(8,128)(2,1)S(1)}, bf16[16,3712]{1,0:T(8,128)(2,1)S(1)}, u32[]{:S(2)}, u32[]{:S(2)}) collective-permute-start(bf16[16,3712]{1,0:T(8,128)(2,1)S(1)} %reshape.110), channel_id=1, source_target_pairs={{0,1},{1,0},{2,3},{3,2},{4,5},{5,4},{6,7},{7,6},{8,9},{9,8},{10,11... | collective-permute-start | bytes 356360 | tf_op jit(solution)/shard_map/ppermute | solution.py:32
  15.4 5.5 %collective-permute-start.4 = (bf16[16,3712]{1,0:T(8,128)(2,1)S(1)}, bf16[16,3712]{1,0:T(8,128)(2,1)S(1)}, u32[]{:S(2)}, u32[]{:S(2)}) collective-permute-start(bf16[16,3712]{1,0:T(8,128)(2,1)S(1)} %reshape.110), channel_id=1, source_target_pairs={{0,4},{1,5},{2,6},{3,7},{4,0},{5,1},{6,2},{7,3},{8,12},{9,13},{10,... | collective-permute-start | bytes 356360 | tf_op jit(solution)/shard_map/ppermute | solution.py:32
  16.9 5.7 %collective-permute-start.5 = (bf16[16,3712]{1,0:T(8,128)(2,1)S(1)}, bf16[16,3712]{1,0:T(8,128)(2,1)S(1)}, u32[]{:S(2)}, u32[]{:S(2)}) collective-permute-start(bf16[16,3712]{1,0:T(8,128)(2,1)S(1)} %reshape.110), channel_id=1, source_target_pairs={{0,5},{1,4},{2,7},{3,6},{4,1},{5,0},{6,3},{7,2},{8,13},{9,12},{10,... | collective-permute-start | bytes 356360 | tf_op jit(solution)/shard_map/ppermute | solution.py:32
  22.7 1.9 %collective-permute-start.6 = (bf16[64,3712]{1,0:T(8,128)(2,1)S(1)}, bf16[64,3712]{1,0:T(8,128)(2,1)S(1)}, u32[]{:S(2)}, u32[]{:S(2)}) collective-permute-start(bf16[64,3712]{1,0:T(8,128)(2,1)S(1)} %pad_maximum_fusion.1.own_ref), channel_id=1, source_target_pairs={{0,2},{1,3},{2,0},{3,1},{4,6},{5,7},{6,4},{7,5},{8,10},{9,11},{10,... | collective-permute-start | bytes 1425416 | tf_op jit(solution)/shard_map/ppermute | solution.py:32
  31.6 3.8 %collective-permute-start.7 = (bf16[64,3584]{1,0:T(8,128)(2,1)S(1)}, bf16[64,3584]{1,0:T(8,128)(2,1)S(1)}, u32[]{:S(2)}, u32[]{:S(2)}) collective-permute-start(bf16[64,3584]{1,0:T(8,128)(2,1)S(1)} %get-tuple-element.10), channel_id=1, source_target_pairs={{0,2},{1,3},{2,0},{3,1},{4,6},{5,7},{6,4},{7,5},{8,10},{9,11},{10,... | collective-permute-start | bytes 1376264 | tf_op jit(solution)/shard_map/ppermute | solution.py:32
  31.9 20.2 %all-to-all-start = ((bf16[16,2,16,576]{3,2,1,0:T(8,128)(2,1)}), bf16[16,2,16,576]{3,2,1,0:T(8,128)(2,1)S(1)}, u32[]{:S(2)}, u32[]{:S(2)}) async-start(bf16[16,2,16,576]{3,2,1,0:T(8,128)(2,1)} %bitcast.8), calls=%async_computation | async-start | bytes 1310720 | tf_op jit(solution)/shard_map/all_to_all | solution.py:199
  35.5 20.8 %copy-start.4 = (bf16[1,2,4,576]{3,2,1,0:T(4,128)(2,1)S(1)}, bf16[1,2,4,576]{3,2,1,0:T(4,128)(2,1)}, u32[]{:S(2)}) copy-start(bf16[1,2,4,576]{3,2,1,0:T(4,128)(2,1)} %param.16) | copy-start | bytes 27652
  52.1 7.6 %collective-permute-start.10 = (bf16[16,3584]{1,0:T(8,128)(2,1)S(1)}, bf16[16,3584]{1,0:T(8,128)(2,1)S(1)}, u32[]{:S(2)}, u32[]{:S(2)}) collective-permute-start(bf16[16,3584]{1,0:T(8,128)(2,1)S(1)} %get-tuple-element.17), channel_id=1, source_target_pairs={{0,5},{1,4},{2,7},{3,6},{4,1},{5,0},{6,3},{7,2},{8,13},{9,12},{10,... | collective-permute-start | bytes 344072 | tf_op jit(solution)/shard_map/ppermute | solution.py:32
  52.8 7.8 %collective-permute-start.8 = (bf16[16,3584]{1,0:T(8,128)(2,1)S(1)}, bf16[16,3584]{1,0:T(8,128)(2,1)S(1)}, u32[]{:S(2)}, u32[]{:S(2)}) collective-permute-start(bf16[16,3584]{1,0:T(8,128)(2,1)S(1)} %get-tuple-element.16), channel_id=1, source_target_pairs={{0,1},{1,0},{2,3},{3,2},{4,5},{5,4},{6,7},{7,6},{8,9},{9,8},{10,11... | collective-permute-start | bytes 344072 | tf_op jit(solution)/shard_map/ppermute | solution.py:32
  54.3 6.3 %collective-permute-start.9 = (bf16[16,3584]{1,0:T(8,128)(2,1)S(1)}, bf16[16,3584]{1,0:T(8,128)(2,1)S(1)}, u32[]{:S(2)}, u32[]{:S(2)}) collective-permute-start(bf16[16,3584]{1,0:T(8,128)(2,1)S(1)} %get-tuple-element.18), channel_id=1, source_target_pairs={{0,4},{1,5},{2,6},{3,7},{4,0},{5,1},{6,2},{7,3},{8,12},{9,13},{10,... | collective-permute-start | bytes 344072 | tf_op jit(solution)/shard_map/ppermute | solution.py:32
  56.3 2.6 %copy-start.3 = (bf16[1,2,4,64,576]{4,3,2,1,0:T(8,128)(2,1)S(1)}, bf16[1,2,4,64,576]{4,3,2,1,0:T(8,128)(2,1)}, u32[]{:S(2)}) copy-start(bf16[1,2,4,64,576]{4,3,2,1,0:T(8,128)(2,1)} %param.17) | copy-start | bytes 1769476
  60.7 8.1 %collective-permute-start.11 = (bf16[4,3584]{1,0:T(4,128)(2,1)S(1)}, bf16[4,3584]{1,0:T(4,128)(2,1)S(1)}, u32[]{:S(2)}, u32[]{:S(2)}) collective-permute-start(bf16[4,3584]{1,0:T(4,128)(2,1)S(1)} %get-tuple-element.19), channel_id=1, source_target_pairs={{0,8},{1,9},{2,10},{3,11},{4,12},{5,13},{6,14},{7,15},{8,0},{9,1},... | collective-permute-start | bytes 86024 | tf_op jit(solution)/shard_map/ppermute | solution.py:32
  63.0 5.8 %collective-permute-start.12 = (bf16[4,3584]{1,0:T(4,128)(2,1)S(1)}, bf16[4,3584]{1,0:T(4,128)(2,1)S(1)}, u32[]{:S(2)}, u32[]{:S(2)}) collective-permute-start(bf16[4,3584]{1,0:T(4,128)(2,1)S(1)} %get-tuple-element.21), channel_id=1, source_target_pairs={{0,16},{1,17},{2,18},{3,19},{4,20},{5,21},{6,22},{7,23},{8,24},{9,... | collective-permute-start | bytes 86024 | tf_op jit(solution)/shard_map/ppermute | solution.py:32
  64.0 5.7 %collective-permute-start.13 = (bf16[4,3584]{1,0:T(4,128)(2,1)S(1)}, bf16[4,3584]{1,0:T(4,128)(2,1)S(1)}, u32[]{:S(2)}, u32[]{:S(2)}) collective-permute-start(bf16[4,3584]{1,0:T(4,128)(2,1)S(1)} %get-tuple-element.20), channel_id=1, source_target_pairs={{0,24},{1,25},{2,26},{3,27},{4,28},{5,29},{6,30},{7,31},{8,16},{9,... | collective-permute-start | bytes 86024 | tf_op jit(solution)/shard_map/ppermute | solution.py:32
where the time goes:
time: 70.7 us; the launch traced here: 70.3 us
  waiting for transfers between devices  28.6 us (40%)
  starting transfers between devices  21.4 us (30%)
  Pallas kernels  7.02 us (10%)
  matrix products  6.66 us (9%)
  other arithmetic  3.51 us (5%)
  local copies, waits for them, and re-layouts  2.36 us (3%)
  between operations  0.8 us (1%)
    ppermute x14, starting transfers between devices, exchange(): return lax.ppermute(value, RANK, [(at, at ^ mask) for at in range(count)])  17.8 us
    all_to_all x1, waiting for transfers between devices, body(): lax.all_to_all(picked_pages.reshape(peers, capp, page_len, width_lat), 'd...  16.4 us
    ppermute x14, waiting for transfers between devices, exchange(): return lax.ppermute(value, RANK, [(at, at ^ mask) for at in range(count)])  12.2 us
    pallas_call x1, Pallas kernels, experts_of(): pl.pallas_call(experts_kernel, out_shape=(half, half), in_specs=[pl.Block...  7.02 us
    all_to_all x1, starting transfers between devices, body(): lax.all_to_all(picked_pages.reshape(peers, capp, page_len, width_lat), 'd...  3.6 us
    dot_general x1, matrix products, attend(): jnp.einsum('rshk,rkv->rshv', weights, values, preferred_element_type=jnp....  3.31 us
    dot_general x1, matrix products, attend(): jnp.einsum('rshl,rkl->rshk', queries, keys, preferred_element_type=jnp.fl...  2.6 us
    gather x1, local copies, waits for them, and re-layouts, body(): picked_pages = pages[jnp.maximum(outgoing_slots, 0)]  1.48 us
  transfers between devices with their start and end apart: 15, of which 9 were waited for; matrix products, arithmetic and copies ran while one was open for 14% of the time, Pallas kernels for 0%

commit v1 on v0

--- a/solution.py
+++ b/solution.py
@@ -1,3 +1,4 @@
+import functools
 import jax
 import jax.numpy as jnp
 from jax import lax
@@ -138,6 +139,31 @@
     )(scalars, own, got, expert_gate, expert_up, expert_down)
 
 
+def pick_kernel(capp, me_ref, send_ref, pages_ref, out_ref, sems):
+    copies = []
+    for at in range(out_ref.shape[0]):
+        slot = ((at // capp) ^ me_ref[0]) * capp + at % capp
+        page = jnp.maximum(send_ref[slot], 0)
+        copies.append(pltpu.make_async_copy(pages_ref.at[page], out_ref.at[at], sems.at[at]))
+        copies[-1].start()
+    for copy in copies:
+        copy.wait()
+
+
+def pick_pages(pages, outgoing_slots, me, capp):
+    slots = outgoing_slots.shape[0]
+    smem = pl.BlockSpec(memory_space=pltpu.SMEM)
+    return pl.pallas_call(
+        functools.partial(pick_kernel, capp),
+        out_shape=jax.ShapeDtypeStruct((slots,) + pages.shape[1:], pages.dtype),
+        in_specs=[smem, smem, pl.BlockSpec(memory_space=pl.ANY)],
+        out_specs=pl.BlockSpec(memory_space=pltpu.VMEM),
+        scratch_shapes=[pltpu.SemaphoreType.DMA((slots,))],
+        cost_estimate=pl.CostEstimate(flops=0, bytes_accessed=4 * pages[0].size * slots, transcendentals=0),
+        name="pick",
+    )(me.reshape(1), outgoing_slots, pages)
+
+
 def attend(queries, new_latent, cache, lengths):
     steps = queries.shape[1]
     ctx = cache.shape[1]
@@ -177,7 +203,8 @@
     outgoing_slots = send_page[0]
     page_len, width_lat = (pages.shape[1], pages.shape[2])
     capp = outgoing_slots.shape[0] // peers
-    picked_pages = pages[jnp.maximum(outgoing_slots, 0)]
+    me = lax.axis_index("dev")
+    sent_pages = pick_pages(pages, outgoing_slots, me, capp)
     owned = expert_gate.shape[0]
     experts = peers * owned
     rows = routing.shape[1]
@@ -189,35 +216,46 @@
     extra = jnp.concatenate([high, low], axis=1)
     pad = -extra.shape[1] % 128
     packed = jnp.concatenate([moe_rows[0], jnp.pad(extra, ((0, 0), (0, pad)))], axis=1)
-    far, near, last = levels_of(peers, lax.axis_size(("section", "tp")))
+    blocks = lax.axis_size(("section", "tp"))
+    far, near, last = levels_of(peers, blocks)
+    low = blocks.bit_length() - 1
+    middle = near[low:]
+    ends = [1 << len(far), 1 << len(middle), 1 << len(last)]
+    moving = sent_pages.reshape(ends + [-1, width_lat])
+    for bit in middle:
+        moving = jnp.stack([moving[:, 0], exchange(moving[:, 1], 1 << bit)], axis=1)
     pooled = packed[None]
     for bits in pairs_of(far):
         pooled = jnp.concatenate([pooled] + [exchange(pooled, mask) for mask in masks_of(bits)[1:]], axis=0)
-    pooled = lax.optimization_barrier(pooled).reshape(-1, packed.shape[1])
-    pooled, picked_pages = lax.optimization_barrier((pooled, picked_pages))
+    pooled, moving = lax.optimization_barrier((pooled, moving))
+    pooled = pooled.reshape(-1, packed.shape[1])
+    masks = masks_of(far)
+    early = [exchange(moving[turn], masks[turn]) for turn in range(1, len(masks) - 1)]
     pooled = jnp.concatenate([pooled] + [exchange(pooled, mask) for mask in masks_of(near)[1:]], axis=0)
-    arrived = lax.all_to_all(
-        picked_pages.reshape(peers, capp, page_len, width_lat),
-        "dev",
-        split_axis=0,
-        concat_axis=0,
-        tiled=True,
-    )
-    arrived = arrived.reshape(peers * capp, page_len, width_lat)
-    pooled = lax.optimization_barrier(pooled)
+    pooled, early, moving = lax.optimization_barrier((pooled, early, moving))
+    late = [exchange(moving[turn], masks[turn]) for turn in range(max(1, len(masks) - 1), len(masks))]
     other = masks_of(last)[-1]
-    first = lax.axis_index("dev") * owned
+    first = me * owned
     kept, sent = experts_of(
         pooled, exchange(pooled, other), first, experts, expert_gate, expert_up, expert_down
     )
+    kept, sent, late = lax.optimization_barrier((kept, sent, late))
     mixed = kept.astype(jnp.float32) + exchange(sent, other).astype(jnp.float32)
-    mixed, arrived = lax.optimization_barrier((mixed.astype(jnp.bfloat16), arrived))
-    for bits in [near] + pairs_of(far)[::-1]:
+    mixed, late = lax.optimization_barrier((mixed.astype(jnp.bfloat16), late))
+    moving = jnp.stack([moving[0]] + list(early) + list(late), axis=0)
+    for bit in last:
+        moving = jnp.stack([moving[:, :, 0], exchange(moving[:, :, 1], 1 << bit)], axis=2)
+    mixed = collect(mixed, near)
+    mixed, moving = lax.optimization_barrier((mixed, moving))
+    for bits in pairs_of(far)[::-1]:
         mixed = collect(mixed, bits)
+    arrived = moving.reshape(peers * capp, page_len, width_lat)
 
     table = page_table[0]
     requests, most_pages = table.shape
-    cache = arrived[jnp.maximum(table, 0)].reshape(requests, most_pages * page_len, width_lat)
+    slots = jnp.maximum(table, 0)
+    slots = ((slots // capp) ^ me) * capp + slots % capp
+    cache = arrived[slots].reshape(requests, most_pages * page_len, width_lat)
     attended = attend(queries[0], new_latent[0], cache, context_len[0])
     return (attended[None], mixed[None])
 

time: 70.7 us -> 66.7 us (0.943)
  waiting for transfers between devices: 28.6 us -> 21.5 us
  starting transfers between devices: 21.4 us -> 25.7 us
  matrix products: 6.66 us -> 3.24 us
  Pallas kernels: 7.02 us -> 9.87 us
    all_to_all x1 -> x0, waiting for transfers between devices: 16.4 us -> none  [body(): lax.all_to_all(picked_pages.reshape(peers, capp, page_len, width_lat), 'd...]
    ppermute x14 -> x19, waiting for transfers between devices: 12.2 us -> 21.5 us  [exchange(): return lax.ppermute(value, RANK, [(at, at ^ mask) for at in range(count)])]
    ppermute x14 -> x19, starting transfers between devices: 17.8 us -> 25.7 us  [exchange(): return lax.ppermute(value, RANK, [(at, at ^ mask) for at in range(count)])]
    all_to_all x1 -> x0, starting transfers between devices: 3.6 us -> none  [body(): lax.all_to_all(picked_pages.reshape(peers, capp, page_len, width_lat), 'd...]
    pallas_call x0 -> x1, Pallas kernels: none -> 2.85 us  [pick_pages(): pl.pallas_call(functools.partial(pick_kernel, capp), out_shape=jax.ShapeD...]
    dot_general x1, matrix products: 2.6 us -> 0.56 us  [attend(): jnp.einsum('rshl,rkl->rshk', queries, keys, preferred_element_type=jnp.fl...]
    gather x2 -> x1, local copies, waits for them, and re-layouts: 2.15 us -> 0.67 us  [body(): cache = arrived[slots].reshape(requests, most_pages * page_len, width_lat)]
    dot_general x1, matrix products: 3.31 us -> 1.94 us  [attend(): jnp.einsum('rshk,rkv->rshv', weights, values, preferred_element_type=jnp....]
  transfers between devices with their start and end apart: 15 -> 19, of which waited for: 9 -> 10; matrix products, arithmetic and copies ran while one was open for 14% -> 6% of each run, Pallas kernels for 0% -> 15%
where the time goes in v1:
time: 66.7 us; the launch traced here: 66.5 us
  starting transfers between devices  25.7 us (39%)
  waiting for transfers between devices  21.5 us (32%)
  Pallas kernels  9.87 us (15%)
  matrix products  3.24 us (5%)
  other arithmetic  3.18 us (5%)
  local copies, waits for them, and re-layouts  2.13 us (3%)
  between operations  0.84 us (1%)
    ppermute x19, starting transfers between devices, exchange(): return lax.ppermute(value, RANK, [(at, at ^ mask) for at in range(count)])  25.7 us
    ppermute x19, waiting for transfers between devices, exchange(): return lax.ppermute(value, RANK, [(at, at ^ mask) for at in range(count)])  21.5 us
    pallas_call x1, Pallas kernels, experts_of(): pl.pallas_call(experts_kernel, out_shape=(half, half), in_specs=[pl.Block...  7.02 us
    pallas_call x1, Pallas kernels, pick_pages(): pl.pallas_call(functools.partial(pick_kernel, capp), out_shape=jax.ShapeD...  2.85 us
    dot_general x1, matrix products, attend(): jnp.einsum('rshk,rkv->rshv', weights, values, preferred_element_type=jnp....  1.94 us
  transfers between devices with their start and end apart: 19, of which 10 were waited for; matrix products, arithmetic and copies ran while one was open for 6% of the time, Pallas kernels for 15%

profile of v1, /device:TPU:0, one launch (start us, length us, event | category | flops | bytes accessed | tf_op | source)
XLA Modules:
  0.0 66.5 jit_solution(10046673824022061005)
XLA Ops:
  0.6 0.8 %select_reduce_fusion = f32[4,16]{1,0:T(4,128)S(1)} fusion(f32[4,8]{1,0:T(4,128)} %bitcast.115, s32[4,8]{1,0:T(4,128)} %bitcast.116), kind=kLoop, calls=%fused_computation.37 | loop fusion | flops 1472 | bytes 512 | tf_op jit(solution)/shard_map/reduce_sum | solution.py:213
  1.6 0.8 %maximum_bitcast_fusion = bf16[1,4,3712]{2,1,0:T(4,128)(2,1)S(1)} fusion(bf16[4,128]{1,0:T(4,128)(2,1)S(1)} %fusion.25, bf16[4,3584]{1,0:T(4,128)(2,1)} %bitcast.114), kind=kLoop, calls=%fused_computation.35 | loop fusion | flops 59392 | bytes 59392 | tf_op jit(solution)/shard_map/broadcast_in_dim | solution.py:227
  2.4 5.1 %collective-permute-start.2 = (bf16[1,4,3712]{2,1,0:T(4,128)(2,1)S(1)}, bf16[1,4,3712]{2,1,0:T(4,128)(2,1)S(1)}, u32[]{:S(2)}, u32[]{:S(2)}) collective-permute-start(bf16[1,4,3712]{2,1,0:T(4,128)(2,1)S(1)} %maximum_bitcast_fusion), channel_id=1, source_target_pairs={{0,24},{1,25},{2,26},{3,27},{4,28},{5,29},{6,30},{7,31},{8,16},{9,... | collective-permute-start | bytes 89096 | tf_op jit(solution)/shard_map/ppermute | solution.py:33
  7.5 0.6 collective-permute-start
  8.1 2.8 %pick.1 = bf16[32,16,576]{2,1,0:T(8,128)(2,1)} custom-call(s32[1]{0:T(128)} %bitcast.1.me_ref, s32[32]{0:T(128)} %bitcast.117, bf16[32,16,576]{2,1,0:T(8,128)(2,1)} %bitcast.105), custom_call_target="tpu_custom_call" | custom-call | bytes 1179648 | tf_op jit(solution)/shard_map/pick/pallas_call | solution.py:156
  11.0 1.1 %slice_bitcast_fusion.3 = (bf16[4,1,2,32,576]{4,3,1,2,0:T(8,128)(2,1)S(1)}, bf16[4,2,32,576]{3,2,1,0:T(8,128)(2,1)S(1)}) fusion(bf16[4,2,2,32,576]{4,3,2,1,0:T(8,128)(2,1)} %bitcast.104), kind=kLoop, calls=%fused_computation.27 | loop fusion | bytes 1179648
  12.1 1.8 %collective-permute-start.3 = (bf16[4,2,32,576]{3,2,1,0:T(8,128)(2,1)S(1)}, bf16[4,2,32,576]{3,2,1,0:T(8,128)(2,1)S(1)}, u32[]{:S(2)}, u32[]{:S(2)}) collective-permute-start(bf16[4,2,32,576]{3,2,1,0:T(8,128)(2,1)S(1)} %get-tuple-element.41), channel_id=1, source_target_pairs={{0,4},{1,5},{2,6},{3,7},{4,0},{5,1},{6,2},{7,3},{8,12},{9,13},{10,... | collective-permute-start | bytes 884744 | tf_op jit(solution)/shard_map/ppermute | solution.py:33
  14.2 6.9 %collective-permute-done.3 = bf16[4,2,32,576]{3,2,1,0:T(8,128)(2,1)S(1)} collective-permute-done((bf16[4,2,32,576]{3,2,1,0:T(8,128)(2,1)S(1)}, bf16[4,2,32,576]{3,2,1,0:T(8,128)(2,1)S(1)}, u32[]{:S(2)}, u32[]{:S(2)}) %collective-permute-start.3) | collective-permute-done | bytes 294944 | tf_op jit(solution)/shard_map/ppermute | solution.py:33
  21.3 2.5 %collective-permute-start.6 = (bf16[16,3712]{1,0:T(8,128)(2,1)S(1)}, bf16[16,3712]{1,0:T(8,128)(2,1)S(1)}, u32[]{:S(2)}, u32[]{:S(2)}) collective-permute-start(bf16[16,3712]{1,0:T(8,128)(2,1)S(1)} %reshape.163), channel_id=1, source_target_pairs={{0,5},{1,4},{2,7},{3,6},{4,1},{5,0},{6,3},{7,2},{8,13},{9,12},{10,... | collective-permute-start | bytes 356360 | tf_op jit(solution)/shard_map/ppermute | solution.py:33
  23.8 0.4 collective-permute-start.5
  24.2 0.6 collective-permute-start.4
  24.9 2.3 %collective-permute-start.8 = (bf16[2,2,32,576]{3,2,0,1:T(8,128)(2,1)S(1)}, bf16[2,2,32,576]{3,2,0,1:T(8,128)(2,1)S(1)}, u32[]{:S(2)}, u32[]{:S(2)}) collective-permute-start(bf16[2,2,32,576]{3,2,0,1:T(8,128)(2,1)S(1)} %get-tuple-element.38), channel_id=1, source_target_pairs={{0,16},{1,17},{2,18},{3,19},{4,20},{5,21},{6,22},{7,23},{8,24},{9,... | collective-permute-start | bytes 442376 | tf_op jit(solution)/shard_map/ppermute | solution.py:33
  27.2 1.7 %collective-permute-start.7 = (bf16[2,2,32,576]{3,2,0,1:T(8,128)(2,1)S(1)}, bf16[2,2,32,576]{3,2,0,1:T(8,128)(2,1)S(1)}, u32[]{:S(2)}, u32[]{:S(2)}) collective-permute-start(bf16[2,2,32,576]{3,2,0,1:T(8,128)(2,1)S(1)} %get-tuple-element.39), channel_id=1, source_target_pairs={{0,8},{1,9},{2,10},{3,11},{4,12},{5,13},{6,14},{7,15},{8,0},{9,1},... | collective-permute-start | bytes 442376 | tf_op jit(solution)/shard_map/ppermute | solution.py:33
  29.2 3.9 %collective-permute-done.8 = bf16[2,2,32,576]{3,2,0,1:T(8,128)(2,1)S(1)} collective-permute-done((bf16[2,2,32,576]{3,2,0,1:T(8,128)(2,1)S(1)}, bf16[2,2,32,576]{3,2,0,1:T(8,128)(2,1)S(1)}, u32[]{:S(2)}, u32[]{:S(2)}) %collective-permute-start.8) | collective-permute-done | bytes 147488 | tf_op jit(solution)/shard_map/ppermute | solution.py:33
  33.4 3.0 %collective-permute-start.10 = (bf16[2,2,32,576]{3,2,0,1:T(8,128)(2,1)S(1)}, bf16[2,2,32,576]{3,2,0,1:T(8,128)(2,1)S(1)}, u32[]{:S(2)}, u32[]{:S(2)}) collective-permute-start(bf16[2,2,32,576]{3,2,0,1:T(8,128)(2,1)S(1)} %get-tuple-element.37), channel_id=1, source_target_pairs={{0,24},{1,25},{2,26},{3,27},{4,28},{5,29},{6,30},{7,31},{8,16},{9,... | collective-permute-start | bytes 442376 | tf_op jit(solution)/shard_map/ppermute | solution.py:33
  36.4 7.0 %experts.1 = (bf16[64,3584]{1,0:T(8,128)(2,1)S(1)}, bf16[64,3584]{1,0:T(8,128)(2,1)S(1)}) custom-call(s32[2]{0:T(128)S(1)} %pad_add_fusion.first_ref, bf16[64,3712]{1,0:T(8,128)(2,1)S(1)} %pad_maximum_fusion.4.own_ref, bf16[64,3712]{1,0:T(8,128)(2,1)S(1)} %collective-permute-done.9.got_ref, bf16[1,3584,512]{2,1,0:T(8,128)(2,1)} %gate_hbm.1, ...), custom_call_target="tpu_custom_call" | custom-call | flops 5637144576 | bytes 11010048 | tf_op jit(solution)/shard_map/experts/pallas_call | solution.py:118
  43.8 1.6 %collective-permute-done.11 = bf16[64,3584]{1,0:T(8,128)(2,1)S(1)} collective-permute-done((bf16[64,3584]{1,0:T(8,128)(2,1)S(1)}, bf16[64,3584]{1,0:T(8,128)(2,1)S(1)}, u32[]{:S(2)}, u32[]{:S(2)}) %collective-permute-start.11) | collective-permute-done | bytes 458784 | tf_op jit(solution)/shard_map/ppermute | solution.py:33
  45.5 1.6 %collective-permute-start.12 = (bf16[16,3584]{1,0:T(8,128)(2,1)S(1)}, bf16[16,3584]{1,0:T(8,128)(2,1)S(1)}, u32[]{:S(2)}, u32[]{:S(2)}) collective-permute-start(bf16[16,3584]{1,0:T(8,128)(2,1)S(1)} %get-tuple-element.42), channel_id=1, source_target_pairs={{0,1},{1,0},{2,3},{3,2},{4,5},{5,4},{6,7},{7,6},{8,9},{9,8},{10,11... | collective-permute-start | bytes 344072 | tf_op jit(solution)/shard_map/ppermute | solution.py:33
  47.1 1.7 %collective-permute-start.14 = (bf16[16,3584]{1,0:T(8,128)(2,1)S(1)}, bf16[16,3584]{1,0:T(8,128)(2,1)S(1)}, u32[]{:S(2)}, u32[]{:S(2)}) collective-permute-start(bf16[16,3584]{1,0:T(8,128)(2,1)S(1)} %get-tuple-element.43), channel_id=1, source_target_pairs={{0,5},{1,4},{2,7},{3,6},{4,1},{5,0},{6,3},{7,2},{8,13},{9,12},{10,... | collective-permute-start | bytes 344072 | tf_op jit(solution)/shard_map/ppermute | solution.py:33
  49.3 1.7 %collective-permute-done.12 = bf16[16,3584]{1,0:T(8,128)(2,1)S(1)} collective-permute-done((bf16[16,3584]{1,0:T(8,128)(2,1)S(1)}, bf16[16,3584]{1,0:T(8,128)(2,1)S(1)}, u32[]{:S(2)}, u32[]{:S(2)}) %collective-permute-start.12) | collective-permute-done | bytes 114720 | tf_op jit(solution)/shard_map/ppermute | solution.py:33
  51.0 3.6 %collective-permute-done.14 = bf16[16,3584]{1,0:T(8,128)(2,1)S(1)} collective-permute-done((bf16[16,3584]{1,0:T(8,128)(2,1)S(1)}, bf16[16,3584]{1,0:T(8,128)(2,1)S(1)}, u32[]{:S(2)}, u32[]{:S(2)}) %collective-permute-start.14) | collective-permute-done | bytes 114720 | tf_op jit(solution)/shard_map/ppermute | solution.py:33
  54.6 1.4 %collective-permute-done.13 = bf16[16,3584]{1,0:T(8,128)(2,1)S(1)} collective-permute-done((bf16[16,3584]{1,0:T(8,128)(2,1)S(1)}, bf16[16,3584]{1,0:T(8,128)(2,1)S(1)}, u32[]{:S(2)}, u32[]{:S(2)}) %collective-permute-start.13) | collective-permute-done | bytes 114720 | tf_op jit(solution)/shard_map/ppermute | solution.py:33
  56.1 0.7 %gather_fusion = bf16[32,16,576]{2,1,0:T(8,128)(2,1)S(1)} fusion(bf16[32,16,576]{2,1,0:T(8,128)(2,1)S(1)} %bitcast.103, s32[1024]{0:T(1024)S(1)} %pad_clamp_fusion), kind=kCustom, calls=%fused_computation | custom fusion | bytes 1179776 | tf_op jit(solution)/shard_map/gather | solution.py:258
  56.8 0.7 %fusion.35 = f32[2,4,64]{2,1,0:T(4,128)S(1)} fusion(bf16[2,4,576]{2,1,0:T(4,128)(2,1)S(1)} %bitcast.119, bf16[1,2,4,64,576]{4,3,2,1,0:T(8,128)(2,1)S(1)} %copy-done, bf16[2,256,576]{2,1,0:T(8,128)(2,1)S(1)} %bitcast.106, pred[2,4,260]{2,1,0:T(4,128)(4,1)S(1)} %broadcast_or_fusion), kind=kOutput, calls=%fused_computation.67 | convolution fusion | flops 155085056 | bytes 1192992 | tf_op jit(solution)/shard_map/sub | solution.py:179
  57.5 0.6 fusion.4
  58.2 1.3 %collective-permute-start.16 = (bf16[4,3584]{1,0:T(4,128)(2,1)S(1)}, bf16[4,3584]{1,0:T(4,128)(2,1)S(1)}, u32[]{:S(2)}, u32[]{:S(2)}) collective-permute-start(bf16[4,3584]{1,0:T(4,128)(2,1)S(1)} %get-tuple-element.45), channel_id=1, source_target_pairs={{0,8},{1,9},{2,10},{3,11},{4,12},{5,13},{6,14},{7,15},{8,0},{9,1},... | collective-permute-start | bytes 86024 | tf_op jit(solution)/shard_map/ppermute | solution.py:33
  59.4 1.7 %collective-permute-start.18 = (bf16[4,3584]{1,0:T(4,128)(2,1)S(1)}, bf16[4,3584]{1,0:T(4,128)(2,1)S(1)}, u32[]{:S(2)}, u32[]{:S(2)}) collective-permute-start(bf16[4,3584]{1,0:T(4,128)(2,1)S(1)} %get-tuple-element.46), channel_id=1, source_target_pairs={{0,24},{1,25},{2,26},{3,27},{4,28},{5,29},{6,30},{7,31},{8,16},{9,... | collective-permute-start | bytes 86024 | tf_op jit(solution)/shard_map/ppermute | solution.py:33
  61.1 0.6 collective-permute-start.17
  61.7 1.9 %fusion.5 = bf16[1,2,4,64,512]{4,3,2,1,0:T(8,128)(2,1)} fusion(bf16[2,256,576]{2,1,0:T(8,128)(2,1)S(1)} %bitcast.108, bf16[2,4,576]{2,1,0:T(4,128)(2,1)S(1)} %bitcast.121, f32[2,4,64]{2,1,0:T(4,128)S(1)} %fusion.35, f32[2,4,64,260]{3,2,1,0:T(8,128)S(1)} %fusion.4), kind=kOutput, calls=%fused_computation.8 | convolution fusion | flops 138042112 | bytes 2766848 | tf_op jit(solution)/shard_map/rshk,rkv->rshv/dot_general | solution.py:182
  63.7 1.4 %collective-permute-done.18 = bf16[4,3584]{1,0:T(4,128)(2,1)S(1)} collective-permute-done((bf16[4,3584]{1,0:T(4,128)(2,1)S(1)}, bf16[4,3584]{1,0:T(4,128)(2,1)S(1)}, u32[]{:S(2)}, u32[]{:S(2)}) %collective-permute-start.18) | collective-permute-done | bytes 28704 | tf_op jit(solution)/shard_map/ppermute | solution.py:33
  65.1 0.8 %collective-permute-done.17 = bf16[4,3584]{1,0:T(4,128)(2,1)S(1)} collective-permute-done((bf16[4,3584]{1,0:T(4,128)(2,1)S(1)}, bf16[4,3584]{1,0:T(4,128)(2,1)S(1)}, u32[]{:S(2)}, u32[]{:S(2)}) %collective-permute-start.17) | collective-permute-done | bytes 28704 | tf_op jit(solution)/shard_map/ppermute | solution.py:33
  65.8 0.6 fusion.14
  (48 shorter events, 2.3 us)
Async XLA Ops:
  0.6 56.2 %copy-start = (bf16[1,2,4,64,576]{4,3,2,1,0:T(8,128)(2,1)S(1)}, bf16[1,2,4,64,576]{4,3,2,1,0:T(8,128)(2,1)}, u32[]{:S(2)}) copy-start(bf16[1,2,4,64,576]{4,3,2,1,0:T(8,128)(2,1)} %param.17) | copy-start | bytes 1769476
  1.5 12.4 %copy-start.1 = (s32[1,2,16]{2,1,0:T(2,128)S(1)}, s32[1,2,16]{2,1,0:T(2,128)}, u32[]{:S(2)}) copy-start(s32[1,2,16]{2,1,0:T(2,128)} %param.14) | copy-start | bytes 388
  2.4 11.7 %collective-permute-start.2 = (bf16[1,4,3712]{2,1,0:T(4,128)(2,1)S(1)}, bf16[1,4,3712]{2,1,0:T(4,128)(2,1)S(1)}, u32[]{:S(2)}, u32[]{:S(2)}) collective-permute-start(bf16[1,4,3712]{2,1,0:T(4,128)(2,1)S(1)} %maximum_bitcast_fusion), channel_id=1, source_target_pairs={{0,24},{1,25},{2,26},{3,27},{4,28},{5,29},{6,30},{7,31},{8,16},{9,... | collective-permute-start | bytes 89096 | tf_op jit(solution)/shard_map/ppermute | solution.py:33
  7.5 6.6 %collective-permute-start.1 = (bf16[1,4,3712]{2,1,0:T(4,128)(2,1)S(1)}, bf16[1,4,3712]{2,1,0:T(4,128)(2,1)S(1)}, u32[]{:S(2)}, u32[]{:S(2)}) collective-permute-start(bf16[1,4,3712]{2,1,0:T(4,128)(2,1)S(1)} %maximum_bitcast_fusion), channel_id=1, source_target_pairs={{0,16},{1,17},{2,18},{3,19},{4,20},{5,21},{6,22},{7,23},{8,24},{9,... | collective-permute-start | bytes 89096 | tf_op jit(solution)/shard_map/ppermute | solution.py:33
  7.5 6.6 %collective-permute-start = (bf16[1,4,3712]{2,1,0:T(4,128)(2,1)S(1)}, bf16[1,4,3712]{2,1,0:T(4,128)(2,1)S(1)}, u32[]{:S(2)}, u32[]{:S(2)}) collective-permute-start(bf16[1,4,3712]{2,1,0:T(4,128)(2,1)S(1)} %maximum_bitcast_fusion), channel_id=1, source_target_pairs={{0,8},{1,9},{2,10},{3,11},{4,12},{5,13},{6,14},{7,15},{8,0},{9,1},... | collective-permute-start | bytes 89096 | tf_op jit(solution)/shard_map/ppermute | solution.py:33
  12.1 9.0 %collective-permute-start.3 = (bf16[4,2,32,576]{3,2,1,0:T(8,128)(2,1)S(1)}, bf16[4,2,32,576]{3,2,1,0:T(8,128)(2,1)S(1)}, u32[]{:S(2)}, u32[]{:S(2)}) collective-permute-start(bf16[4,2,32,576]{3,2,1,0:T(8,128)(2,1)S(1)} %get-tuple-element.41), channel_id=1, source_target_pairs={{0,4},{1,5},{2,6},{3,7},{4,0},{5,1},{6,2},{7,3},{8,12},{9,13},{10,... | collective-permute-start | bytes 884744 | tf_op jit(solution)/shard_map/ppermute | solution.py:33
  21.1 12.2 %copy-start.2 = (s32[1,2]{1,0:T(1,128)S(1)}, s32[1,2]{1,0:T(1,128)}, u32[]{:S(2)}) copy-start(s32[1,2]{1,0:T(1,128)} %param.15) | copy-start | bytes 28
  21.3 7.7 %collective-permute-start.6 = (bf16[16,3712]{1,0:T(8,128)(2,1)S(1)}, bf16[16,3712]{1,0:T(8,128)(2,1)S(1)}, u32[]{:S(2)}, u32[]{:S(2)}) collective-permute-start(bf16[16,3712]{1,0:T(8,128)(2,1)S(1)} %reshape.163), channel_id=1, source_target_pairs={{0,5},{1,4},{2,7},{3,6},{4,1},{5,0},{6,3},{7,2},{8,13},{9,12},{10,... | collective-permute-start | bytes 356360 | tf_op jit(solution)/shard_map/ppermute | solution.py:33
  23.8 5.3 %collective-permute-start.5 = (bf16[16,3712]{1,0:T(8,128)(2,1)S(1)}, bf16[16,3712]{1,0:T(8,128)(2,1)S(1)}, u32[]{:S(2)}, u32[]{:S(2)}) collective-permute-start(bf16[16,3712]{1,0:T(8,128)(2,1)S(1)} %reshape.163), channel_id=1, source_target_pairs={{0,4},{1,5},{2,6},{3,7},{4,0},{5,1},{6,2},{7,3},{8,12},{9,13},{10,... | collective-permute-start | bytes 356360 | tf_op jit(solution)/shard_map/ppermute | solution.py:33
  24.2 4.9 %collective-permute-start.4 = (bf16[16,3712]{1,0:T(8,128)(2,1)S(1)}, bf16[16,3712]{1,0:T(8,128)(2,1)S(1)}, u32[]{:S(2)}, u32[]{:S(2)}) collective-permute-start(bf16[16,3712]{1,0:T(8,128)(2,1)S(1)} %reshape.163), channel_id=1, source_target_pairs={{0,1},{1,0},{2,3},{3,2},{4,5},{5,4},{6,7},{7,6},{8,9},{9,8},{10,11... | collective-permute-start | bytes 356360 | tf_op jit(solution)/shard_map/ppermute | solution.py:33
  24.9 8.3 %collective-permute-start.8 = (bf16[2,2,32,576]{3,2,0,1:T(8,128)(2,1)S(1)}, bf16[2,2,32,576]{3,2,0,1:T(8,128)(2,1)S(1)}, u32[]{:S(2)}, u32[]{:S(2)}) collective-permute-start(bf16[2,2,32,576]{3,2,0,1:T(8,128)(2,1)S(1)} %get-tuple-element.38), channel_id=1, source_target_pairs={{0,16},{1,17},{2,18},{3,19},{4,20},{5,21},{6,22},{7,23},{8,24},{9,... | collective-permute-start | bytes 442376 | tf_op jit(solution)/shard_map/ppermute | solution.py:33
  27.2 6.0 %collective-permute-start.7 = (bf16[2,2,32,576]{3,2,0,1:T(8,128)(2,1)S(1)}, bf16[2,2,32,576]{3,2,0,1:T(8,128)(2,1)S(1)}, u32[]{:S(2)}, u32[]{:S(2)}) collective-permute-start(bf16[2,2,32,576]{3,2,0,1:T(8,128)(2,1)S(1)} %get-tuple-element.39), channel_id=1, source_target_pairs={{0,8},{1,9},{2,10},{3,11},{4,12},{5,13},{6,14},{7,15},{8,0},{9,1},... | collective-permute-start | bytes 442376 | tf_op jit(solution)/shard_map/ppermute | solution.py:33
  33.2 3.2 %collective-permute-start.9 = (bf16[64,3712]{1,0:T(8,128)(2,1)S(1)}, bf16[64,3712]{1,0:T(8,128)(2,1)S(1)}, u32[]{:S(2)}, u32[]{:S(2)}) collective-permute-start(bf16[64,3712]{1,0:T(8,128)(2,1)S(1)} %pad_maximum_fusion.4.own_ref), channel_id=1, source_target_pairs={{0,2},{1,3},{2,0},{3,1},{4,6},{5,7},{6,4},{7,5},{8,10},{9,11},{10,... | collective-permute-start | bytes 1425416 | tf_op jit(solution)/shard_map/ppermute | solution.py:33
  33.4 10.0 %collective-permute-start.10 = (bf16[2,2,32,576]{3,2,0,1:T(8,128)(2,1)S(1)}, bf16[2,2,32,576]{3,2,0,1:T(8,128)(2,1)S(1)}, u32[]{:S(2)}, u32[]{:S(2)}) collective-permute-start(bf16[2,2,32,576]{3,2,0,1:T(8,128)(2,1)S(1)} %get-tuple-element.37), channel_id=1, source_target_pairs={{0,24},{1,25},{2,26},{3,27},{4,28},{5,29},{6,30},{7,31},{8,16},{9,... | collective-permute-start | bytes 442376 | tf_op jit(solution)/shard_map/ppermute | solution.py:33
  43.5 1.9 %collective-permute-start.11 = (bf16[64,3584]{1,0:T(8,128)(2,1)S(1)}, bf16[64,3584]{1,0:T(8,128)(2,1)S(1)}, u32[]{:S(2)}, u32[]{:S(2)}) collective-permute-start(bf16[64,3584]{1,0:T(8,128)(2,1)S(1)} %get-tuple-element.24), channel_id=1, source_target_pairs={{0,2},{1,3},{2,0},{3,1},{4,6},{5,7},{6,4},{7,5},{8,10},{9,11},{10,... | collective-permute-start | bytes 1376264 | tf_op jit(solution)/shard_map/ppermute | solution.py:33
  45.5 5.5 %collective-permute-start.12 = (bf16[16,3584]{1,0:T(8,128)(2,1)S(1)}, bf16[16,3584]{1,0:T(8,128)(2,1)S(1)}, u32[]{:S(2)}, u32[]{:S(2)}) collective-permute-start(bf16[16,3584]{1,0:T(8,128)(2,1)S(1)} %get-tuple-element.42), channel_id=1, source_target_pairs={{0,1},{1,0},{2,3},{3,2},{4,5},{5,4},{6,7},{7,6},{8,9},{9,8},{10,11... | collective-permute-start | bytes 344072 | tf_op jit(solution)/shard_map/ppermute | solution.py:33
  47.1 7.5 %collective-permute-start.14 = (bf16[16,3584]{1,0:T(8,128)(2,1)S(1)}, bf16[16,3584]{1,0:T(8,128)(2,1)S(1)}, u32[]{:S(2)}, u32[]{:S(2)}) collective-permute-start(bf16[16,3584]{1,0:T(8,128)(2,1)S(1)} %get-tuple-element.43), channel_id=1, source_target_pairs={{0,5},{1,4},{2,7},{3,6},{4,1},{5,0},{6,3},{7,2},{8,13},{9,12},{10,... | collective-permute-start | bytes 344072 | tf_op jit(solution)/shard_map/ppermute | solution.py:33
  48.7 7.2 %collective-permute-start.13 = (bf16[16,3584]{1,0:T(8,128)(2,1)S(1)}, bf16[16,3584]{1,0:T(8,128)(2,1)S(1)}, u32[]{:S(2)}, u32[]{:S(2)}) collective-permute-start(bf16[16,3584]{1,0:T(8,128)(2,1)S(1)} %get-tuple-element.44), channel_id=1, source_target_pairs={{0,4},{1,5},{2,6},{3,7},{4,0},{5,1},{6,2},{7,3},{8,12},{9,13},{10,... | collective-permute-start | bytes 344072 | tf_op jit(solution)/shard_map/ppermute | solution.py:33
  49.2 6.7 %collective-permute-start.15 = (bf16[4,2,32,576]{3,2,1,0:T(8,128)(2,1)S(1)}, bf16[4,2,32,576]{3,2,1,0:T(8,128)(2,1)S(1)}, u32[]{:S(2)}, u32[]{:S(2)}) collective-permute-start(bf16[4,2,32,576]{3,2,1,0:T(8,128)(2,1)S(1)} %get-tuple-element.35), channel_id=1, source_target_pairs={{0,2},{1,3},{2,0},{3,1},{4,6},{5,7},{6,4},{7,5},{8,10},{9,11},{10,... | collective-permute-start | bytes 884744 | tf_op jit(solution)/shard_map/ppermute | solution.py:33
  56.0 0.8 %copy-start.3 = (bf16[1,2,4,576]{3,2,1,0:T(4,128)(2,1)S(1)}, bf16[1,2,4,576]{3,2,1,0:T(4,128)(2,1)}, u32[]{:S(2)}) copy-start(bf16[1,2,4,576]{3,2,1,0:T(4,128)(2,1)} %param.16) | copy-start | bytes 27652
  58.2 5.5 %collective-permute-start.16 = (bf16[4,3584]{1,0:T(4,128)(2,1)S(1)}, bf16[4,3584]{1,0:T(4,128)(2,1)S(1)}, u32[]{:S(2)}, u32[]{:S(2)}) collective-permute-start(bf16[4,3584]{1,0:T(4,128)(2,1)S(1)} %get-tuple-element.45), channel_id=1, source_target_pairs={{0,8},{1,9},{2,10},{3,11},{4,12},{5,13},{6,14},{7,15},{8,0},{9,1},... | collective-permute-start | bytes 86024 | tf_op jit(solution)/shard_map/ppermute | solution.py:33
  59.4 5.7 %collective-permute-start.18 = (bf16[4,3584]{1,0:T(4,128)(2,1)S(1)}, bf16[4,3584]{1,0:T(4,128)(2,1)S(1)}, u32[]{:S(2)}, u32[]{:S(2)}) collective-permute-start(bf16[4,3584]{1,0:T(4,128)(2,1)S(1)} %get-tuple-element.46), channel_id=1, source_target_pairs={{0,24},{1,25},{2,26},{3,27},{4,28},{5,29},{6,30},{7,31},{8,16},{9,... | collective-permute-start | bytes 86024 | tf_op jit(solution)/shard_map/ppermute | solution.py:33
  61.1 4.8 %collective-permute-start.17 = (bf16[4,3584]{1,0:T(4,128)(2,1)S(1)}, bf16[4,3584]{1,0:T(4,128)(2,1)S(1)}, u32[]{:S(2)}, u32[]{:S(2)}) collective-permute-start(bf16[4,3584]{1,0:T(4,128)(2,1)S(1)} %get-tuple-element.47), channel_id=1, source_target_pairs={{0,16},{1,17},{2,18},{3,19},{4,20},{5,21},{6,22},{7,23},{8,24},{9,... | collective-permute-start | bytes 86024 | tf_op jit(solution)/shard_map/ppermute | solution.py:33

commit v2 on v0

--- a/solution.py
+++ b/solution.py
@@ -193,8 +193,7 @@
     pooled = packed[None]
     for bits in pairs_of(far):
         pooled = jnp.concatenate([pooled] + [exchange(pooled, mask) for mask in masks_of(bits)[1:]], axis=0)
-    pooled = lax.optimization_barrier(pooled).reshape(-1, packed.shape[1])
-    pooled, picked_pages = lax.optimization_barrier((pooled, picked_pages))
+    pooled = pooled.reshape(-1, packed.shape[1])
     pooled = jnp.concatenate([pooled] + [exchange(pooled, mask) for mask in masks_of(near)[1:]], axis=0)
     arrived = lax.all_to_all(
         picked_pages.reshape(peers, capp, page_len, width_lat),
@@ -204,14 +203,13 @@
         tiled=True,
     )
     arrived = arrived.reshape(peers * capp, page_len, width_lat)
-    pooled = lax.optimization_barrier(pooled)
     other = masks_of(last)[-1]
     first = lax.axis_index("dev") * owned
     kept, sent = experts_of(
         pooled, exchange(pooled, other), first, experts, expert_gate, expert_up, expert_down
     )
     mixed = kept.astype(jnp.float32) + exchange(sent, other).astype(jnp.float32)
-    mixed, arrived = lax.optimization_barrier((mixed.astype(jnp.bfloat16), arrived))
+    mixed = mixed.astype(jnp.bfloat16)
     for bits in [near] + pairs_of(far)[::-1]:
         mixed = collect(mixed, bits)
 

time: 70.7 us -> 60.6 us (0.86)
  waiting for transfers between devices: 28.6 us -> 16.6 us
  starting transfers between devices: 21.4 us -> 23.2 us
    all_to_all x1, waiting for transfers between devices: 16.4 us -> 0.01 us  [body(): lax.all_to_all(picked_pages.reshape(peers, capp, page_len, width_lat), 'd...]
    ppermute x14, waiting for transfers between devices: 12.2 us -> 16.6 us  [exchange(): return lax.ppermute(value, RANK, [(at, at ^ mask) for at in range(count)])]
    all_to_all x1, starting transfers between devices: 3.6 us -> 6.21 us  [body(): lax.all_to_all(picked_pages.reshape(peers, capp, page_len, width_lat), 'd...]
    ppermute x14, starting transfers between devices: 17.8 us -> 17 us  [exchange(): return lax.ppermute(value, RANK, [(at, at ^ mask) for at in range(count)])]
  transfers between devices with their start and end apart: 15 -> 15, of which waited for: 9 -> 7; matrix products, arithmetic and copies ran while one was open for 14% -> 17% of each run, Pallas kernels for 0% -> 12%
where the time goes in v2:
time: 60.6 us; the launch traced here: 60.2 us
  starting transfers between devices  23.2 us (38%)
  waiting for transfers between devices  16.6 us (27%)
  Pallas kernels  7.02 us (12%)
  matrix products  6.66 us (11%)
  other arithmetic  3.47 us (6%)
  local copies, waits for them, and re-layouts  2.41 us (4%)
  between operations  0.83 us (1%)
    ppermute x14, starting transfers between devices, exchange(): return lax.ppermute(value, RANK, [(at, at ^ mask) for at in range(count)])  17 us
    ppermute x14, waiting for transfers between devices, exchange(): return lax.ppermute(value, RANK, [(at, at ^ mask) for at in range(count)])  16.6 us
    pallas_call x1, Pallas kernels, experts_of(): pl.pallas_call(experts_kernel, out_shape=(half, half), in_specs=[pl.Block...  7.02 us
    all_to_all x1, starting transfers between devices, body(): lax.all_to_all(picked_pages.reshape(peers, capp, page_len, width_lat), 'd...  6.21 us
    dot_general x1, matrix products, attend(): jnp.einsum('rshk,rkv->rshv', weights, values, preferred_element_type=jnp....  3.31 us
    dot_general x1, matrix products, attend(): jnp.einsum('rshl,rkl->rshk', queries, keys, preferred_element_type=jnp.fl...  2.6 us
    gather x1, local copies, waits for them, and re-layouts, body(): picked_pages = pages[jnp.maximum(outgoing_slots, 0)]  1.48 us
  transfers between devices with their start and end apart: 15, of which 7 were waited for; matrix products, arithmetic and copies ran while one was open for 17% of the time, Pallas kernels for 12%

profile of v2, /device:TPU:0, one launch (start us, length us, event | category | flops | bytes accessed | tf_op | source)
XLA Modules:
  0.0 60.2 jit_solution(10727501761642303079)
XLA Ops:
  0.6 0.8 %select_reduce_fusion = f32[4,16]{1,0:T(4,128)S(1)} fusion(f32[4,8]{1,0:T(4,128)} %bitcast.54, s32[4,8]{1,0:T(4,128)} %bitcast.55), kind=kLoop, calls=%fused_computation.26 | loop fusion | flops 1472 | bytes 512 | tf_op jit(solution)/shard_map/reduce_sum | solution.py:186
  1.6 0.8 %maximum_bitcast_fusion = bf16[1,4,3712]{2,1,0:T(4,128)(2,1)S(1)} fusion(bf16[4,128]{1,0:T(4,128)(2,1)S(1)} %fusion.22, bf16[4,3584]{1,0:T(4,128)(2,1)} %bitcast.53), kind=kLoop, calls=%fused_computation.24 | loop fusion | flops 59392 | bytes 59392 | tf_op jit(solution)/shard_map/broadcast_in_dim | solution.py:193
  2.4 5.1 %collective-permute-start.2 = (bf16[1,4,3712]{2,1,0:T(4,128)(2,1)S(1)}, bf16[1,4,3712]{2,1,0:T(4,128)(2,1)S(1)}, u32[]{:S(2)}, u32[]{:S(2)}) collective-permute-start(bf16[1,4,3712]{2,1,0:T(4,128)(2,1)S(1)} %maximum_bitcast_fusion), channel_id=1, source_target_pairs={{0,24},{1,25},{2,26},{3,27},{4,28},{5,29},{6,30},{7,31},{8,16},{9,... | collective-permute-start | bytes 89096 | tf_op jit(solution)/shard_map/ppermute | solution.py:32
  7.5 0.6 %collective-permute-start = (bf16[1,4,3712]{2,1,0:T(4,128)(2,1)S(1)}, bf16[1,4,3712]{2,1,0:T(4,128)(2,1)S(1)}, u32[]{:S(2)}, u32[]{:S(2)}) collective-permute-start(bf16[1,4,3712]{2,1,0:T(4,128)(2,1)S(1)} %maximum_bitcast_fusion), channel_id=1, source_target_pairs={{0,8},{1,9},{2,10},{3,11},{4,12},{5,13},{6,14},{7,15},{8,0},{9,1},... | collective-permute-start | bytes 89096 | tf_op jit(solution)/shard_map/ppermute | solution.py:32
  8.1 0.7 %maximum_bitcast_fusion.1 = s32[32]{0:T(128)S(1)} fusion(s32[1,32]{1,0:T(1,128)} %param.13), kind=kLoop, calls=%fused_computation.47 | loop fusion | flops 32 | bytes 256 | tf_op jit(solution)/shard_map/max | solution.py:180
  8.8 1.5 %gather_fusion = bf16[32,16,576]{2,1,0:T(8,128)(2,1)} fusion(bf16[32,16,576]{2,1,0:T(8,128)(2,1)S(1)} %bitcast.48, s32[1024]{0:T(1024)S(1)} %pad_clamp_fusion.1), kind=kCustom, calls=%fused_computation | custom fusion | bytes 1179776 | tf_op jit(solution)/shard_map/gather | solution.py:180
  10.3 6.2 %all-to-all-start = ((bf16[16,2,16,576]{3,2,1,0:T(8,128)(2,1)}), bf16[16,2,16,576]{3,2,1,0:T(8,128)(2,1)S(1)}, u32[]{:S(2)}, u32[]{:S(2)}) async-start(bf16[16,2,16,576]{3,2,1,0:T(8,128)(2,1)} %bitcast.3), calls=%async_computation | async-start | bytes 1310720 | tf_op jit(solution)/shard_map/all_to_all | solution.py:198
  16.5 0.1 pad_maximum_fusion.1
  16.7 2.9 %collective-permute-start.5 = (bf16[16,3712]{1,0:T(8,128)(2,1)S(1)}, bf16[16,3712]{1,0:T(8,128)(2,1)S(1)}, u32[]{:S(2)}, u32[]{:S(2)}) collective-permute-start(bf16[16,3712]{1,0:T(8,128)(2,1)S(1)} %reshape.113), channel_id=1, source_target_pairs={{0,5},{1,4},{2,7},{3,6},{4,1},{5,0},{6,3},{7,2},{8,13},{9,12},{10,... | collective-permute-start | bytes 356360 | tf_op jit(solution)/shard_map/ppermute | solution.py:32
  19.6 0.1 collective-permute-start.4
  19.7 0.5 collective-permute-start.3
  20.3 5.9 %collective-permute-done.3 = bf16[16,3712]{1,0:T(8,128)(2,1)S(1)} collective-permute-done((bf16[16,3712]{1,0:T(8,128)(2,1)S(1)}, bf16[16,3712]{1,0:T(8,128)(2,1)S(1)}, u32[]{:S(2)}, u32[]{:S(2)}) %collective-permute-start.3) | collective-permute-done | bytes 118816 | tf_op jit(solution)/shard_map/ppermute | solution.py:32
  26.2 3.8 %collective-permute-done.4 = bf16[16,3712]{1,0:T(8,128)(2,1)S(1)} collective-permute-done((bf16[16,3712]{1,0:T(8,128)(2,1)S(1)}, bf16[16,3712]{1,0:T(8,128)(2,1)S(1)}, u32[]{:S(2)}, u32[]{:S(2)}) %collective-permute-start.4) | collective-permute-done | bytes 118816 | tf_op jit(solution)/shard_map/ppermute | solution.py:32
  30.4 1.6 %collective-permute-done.6.got_ref = bf16[64,3712]{1,0:T(8,128)(2,1)S(1)} collective-permute-done((bf16[64,3712]{1,0:T(8,128)(2,1)S(1)}, bf16[64,3712]{1,0:T(8,128)(2,1)S(1)}, u32[]{:S(2)}, u32[]{:S(2)}) %collective-permute-start.6) | collective-permute-done | bytes 475168 | tf_op jit(solution)/shard_map/ppermute | solution.py:32
  31.9 7.0 %experts.1 = (bf16[64,3584]{1,0:T(8,128)(2,1)S(1)}, bf16[64,3584]{1,0:T(8,128)(2,1)S(1)}) custom-call(s32[2]{0:T(128)S(1)} %pad_add_fusion.first_ref, bf16[64,3712]{1,0:T(8,128)(2,1)S(1)} %constant_dynamic-update-slice_fusion.own_ref, bf16[64,3712]{1,0:T(8,128)(2,1)S(1)} %collective-permute-done.6.got_ref, bf16[1,3584,512]{2,1,0:T(8,128)(2,1)} %gate_hbm.1, ...), custom_call_target="tpu_custom_call" | custom-call | flops 5637144576 | bytes 11010048 | tf_op jit(solution)/shard_map/experts/pallas_call | solution.py:117
  39.0 0.2 collective-permute-start.7
  39.2 1.6 %collective-permute-done.7 = bf16[64,3584]{1,0:T(8,128)(2,1)S(1)} collective-permute-done((bf16[64,3584]{1,0:T(8,128)(2,1)S(1)}, bf16[64,3584]{1,0:T(8,128)(2,1)S(1)}, u32[]{:S(2)}, u32[]{:S(2)}) %collective-permute-start.7) | collective-permute-done | bytes 458784 | tf_op jit(solution)/shard_map/ppermute | solution.py:32
  40.8 0.1 add_convert_fusion
  41.0 1.6 %collective-permute-start.8 = (bf16[16,3584]{1,0:T(8,128)(2,1)S(1)}, bf16[16,3584]{1,0:T(8,128)(2,1)S(1)}, u32[]{:S(2)}, u32[]{:S(2)}) collective-permute-start(bf16[16,3584]{1,0:T(8,128)(2,1)S(1)} %get-tuple-element.8), channel_id=1, source_target_pairs={{0,1},{1,0},{2,3},{3,2},{4,5},{5,4},{6,7},{7,6},{8,9},{9,8},{10,11... | collective-permute-start | bytes 344072 | tf_op jit(solution)/shard_map/ppermute | solution.py:32
  42.5 1.5 %collective-permute-start.10 = (bf16[16,3584]{1,0:T(8,128)(2,1)S(1)}, bf16[16,3584]{1,0:T(8,128)(2,1)S(1)}, u32[]{:S(2)}, u32[]{:S(2)}) collective-permute-start(bf16[16,3584]{1,0:T(8,128)(2,1)S(1)} %get-tuple-element.9), channel_id=1, source_target_pairs={{0,5},{1,4},{2,7},{3,6},{4,1},{5,0},{6,3},{7,2},{8,13},{9,12},{10,... | collective-permute-start | bytes 344072 | tf_op jit(solution)/shard_map/ppermute | solution.py:32
  44.0 0.5 collective-permute-start.9
  44.5 0.7 %gather_fusion.1 = bf16[32,16,576]{2,1,0:T(8,128)(2,1)S(1)} fusion(bf16[32,16,576]{2,1,0:T(8,128)(2,1)S(1)} %bitcast.49, s32[1024]{0:T(1024)S(1)} %pad_clamp_fusion), kind=kCustom, calls=%fused_computation.1 | custom fusion | bytes 1179776 | tf_op jit(solution)/shard_map/gather | solution.py:218
  45.2 2.6 %fusion.4 = f32[2,4,64,260]{3,2,1,0:T(8,128)} fusion(bf16[2,4,576]{2,1,0:T(4,128)(2,1)S(1)} %bitcast.57, bf16[1,2,4,64,576]{4,3,2,1,0:T(8,128)(2,1)} %param.17, bf16[2,256,576]{2,1,0:T(8,128)(2,1)S(1)} %bitcast.50, pred[2,4,260]{2,1,0:T(4,128)(4,1)S(1)} %broadcast_or_fusion), kind=kOutput, calls=%fused_computation.8 | convolution fusion | flops 154818560 | bytes 1723424 | tf_op jit(solution)/shard_map/rshl,rkl->rshk/dot_general | solution.py:145
  47.8 0.8 %fusion.32 = f32[2,4,64]{2,1,0:T(4,128)S(1)} fusion(bf16[2,4,576]{2,1,0:T(4,128)(2,1)S(1)} %bitcast.58, bf16[1,2,4,64,576]{4,3,2,1,0:T(8,128)(2,1)S(1)} %copy-done.3, bf16[2,256,576]{2,1,0:T(8,128)(2,1)S(1)} %bitcast.51, pred[2,4,260]{2,1,0:T(4,128)(4,1)S(1)} %broadcast_or_fusion), kind=kOutput, calls=%fused_computation.56 | convolution fusion | flops 155085056 | bytes 1192992 | tf_op jit(solution)/shard_map/sub | solution.py:153
  48.6 1.2 %collective-permute-done.10 = bf16[16,3584]{1,0:T(8,128)(2,1)S(1)} collective-permute-done((bf16[16,3584]{1,0:T(8,128)(2,1)S(1)}, bf16[16,3584]{1,0:T(8,128)(2,1)S(1)}, u32[]{:S(2)}, u32[]{:S(2)}) %collective-permute-start.10) | collective-permute-done | bytes 114720 | tf_op jit(solution)/shard_map/ppermute | solution.py:32
  49.8 1.4 %collective-permute-done.9 = bf16[16,3584]{1,0:T(8,128)(2,1)S(1)} collective-permute-done((bf16[16,3584]{1,0:T(8,128)(2,1)S(1)}, bf16[16,3584]{1,0:T(8,128)(2,1)S(1)}, u32[]{:S(2)}, u32[]{:S(2)}) %collective-permute-start.9) | collective-permute-done | bytes 114720 | tf_op jit(solution)/shard_map/ppermute | solution.py:32
  51.2 1.2 %collective-permute-start.11 = (bf16[4,3584]{1,0:T(4,128)(2,1)S(1)}, bf16[4,3584]{1,0:T(4,128)(2,1)S(1)}, u32[]{:S(2)}, u32[]{:S(2)}) collective-permute-start(bf16[4,3584]{1,0:T(4,128)(2,1)S(1)} %get-tuple-element.11), channel_id=1, source_target_pairs={{0,8},{1,9},{2,10},{3,11},{4,12},{5,13},{6,14},{7,15},{8,0},{9,1},... | collective-permute-start | bytes 86024 | tf_op jit(solution)/shard_map/ppermute | solution.py:32
  52.4 2.4 %collective-permute-start.13 = (bf16[4,3584]{1,0:T(4,128)(2,1)S(1)}, bf16[4,3584]{1,0:T(4,128)(2,1)S(1)}, u32[]{:S(2)}, u32[]{:S(2)}) collective-permute-start(bf16[4,3584]{1,0:T(4,128)(2,1)S(1)} %get-tuple-element.12), channel_id=1, source_target_pairs={{0,24},{1,25},{2,26},{3,27},{4,28},{5,29},{6,30},{7,31},{8,16},{9,... | collective-permute-start | bytes 86024 | tf_op jit(solution)/shard_map/ppermute | solution.py:32
  54.8 0.3 collective-permute-start.12
  55.1 3.3 %fusion.5 = bf16[1,2,4,64,512]{4,3,2,1,0:T(8,128)(2,1)} fusion(bf16[2,256,576]{2,1,0:T(8,128)(2,1)S(1)} %bitcast.52, bf16[2,4,576]{2,1,0:T(4,128)(2,1)S(1)} %bitcast.59, f32[2,4,64]{2,1,0:T(4,128)S(1)} %fusion.32, f32[2,4,64,260]{3,2,1,0:T(8,128)} %fusion.4), kind=kOutput, calls=%fused_computation.9 | convolution fusion | flops 138042112 | bytes 2698240 | tf_op jit(solution)/shard_map/rshk,rkv->rshv/dot_general | solution.py:156
  58.4 1.2 %collective-permute-done.12 = bf16[4,3584]{1,0:T(4,128)(2,1)S(1)} collective-permute-done((bf16[4,3584]{1,0:T(4,128)(2,1)S(1)}, bf16[4,3584]{1,0:T(4,128)(2,1)S(1)}, u32[]{:S(2)}, u32[]{:S(2)}) %collective-permute-start.12) | collective-permute-done | bytes 28704 | tf_op jit(solution)/shard_map/ppermute | solution.py:32
  59.6 0.6 %fusion.14 = bf16[1,4,3584]{2,1,0:T(4,128)(2,1)} fusion(bf16[4,3584]{1,0:T(4,128)(2,1)S(1)} %collective-permute-done.13, bf16[4,3584]{1,0:T(4,128)(2,1)S(1)} %collective-permute-done.12, bf16[4,3584]{1,0:T(4,128)(2,1)S(1)} %collective-permute-done.11, bf16[16,3584]{1,0:T(8,128)(2,1)S(1)} %add_convert_fusion.1), kind=kLoop, calls=%fused_computation.25 | loop fusion | flops 114688 | bytes 143360 | tf_op jit(solution)/shard_map/broadcast_in_dim | solution.py:220
  (40 shorter events, 0.7 us)
Async XLA Ops:
  0.6 8.2 %copy-start = (bf16[1,32,16,576]{3,2,1,0:T(8,128)(2,1)S(1)}, bf16[1,32,16,576]{3,2,1,0:T(8,128)(2,1)}, u32[]{:S(2)}) copy-start(bf16[1,32,16,576]{3,2,1,0:T(8,128)(2,1)} %param.12) | copy-start | bytes 1769476
  1.5 15.0 %copy-start.1 = (s32[1,2,16]{2,1,0:T(2,128)S(1)}, s32[1,2,16]{2,1,0:T(2,128)}, u32[]{:S(2)}) copy-start(s32[1,2,16]{2,1,0:T(2,128)} %param.14) | copy-start | bytes 388
  2.4 14.2 %collective-permute-start.2 = (bf16[1,4,3712]{2,1,0:T(4,128)(2,1)S(1)}, bf16[1,4,3712]{2,1,0:T(4,128)(2,1)S(1)}, u32[]{:S(2)}, u32[]{:S(2)}) collective-permute-start(bf16[1,4,3712]{2,1,0:T(4,128)(2,1)S(1)} %maximum_bitcast_fusion), channel_id=1, source_target_pairs={{0,24},{1,25},{2,26},{3,27},{4,28},{5,29},{6,30},{7,31},{8,16},{9,... | collective-permute-start | bytes 89096 | tf_op jit(solution)/shard_map/ppermute | solution.py:32
  7.5 9.1 %collective-permute-start.1 = (bf16[1,4,3712]{2,1,0:T(4,128)(2,1)S(1)}, bf16[1,4,3712]{2,1,0:T(4,128)(2,1)S(1)}, u32[]{:S(2)}, u32[]{:S(2)}) collective-permute-start(bf16[1,4,3712]{2,1,0:T(4,128)(2,1)S(1)} %maximum_bitcast_fusion), channel_id=1, source_target_pairs={{0,16},{1,17},{2,18},{3,19},{4,20},{5,21},{6,22},{7,23},{8,24},{9,... | collective-permute-start | bytes 89096 | tf_op jit(solution)/shard_map/ppermute | solution.py:32
  7.5 9.1 %collective-permute-start = (bf16[1,4,3712]{2,1,0:T(4,128)(2,1)S(1)}, bf16[1,4,3712]{2,1,0:T(4,128)(2,1)S(1)}, u32[]{:S(2)}, u32[]{:S(2)}) collective-permute-start(bf16[1,4,3712]{2,1,0:T(4,128)(2,1)S(1)} %maximum_bitcast_fusion), channel_id=1, source_target_pairs={{0,8},{1,9},{2,10},{3,11},{4,12},{5,13},{6,14},{7,15},{8,0},{9,1},... | collective-permute-start | bytes 89096 | tf_op jit(solution)/shard_map/ppermute | solution.py:32
  10.3 20.0 %copy-start.2 = (s32[1,2]{1,0:T(1,128)S(1)}, s32[1,2]{1,0:T(1,128)}, u32[]{:S(2)}) copy-start(s32[1,2]{1,0:T(1,128)} %param.15) | copy-start | bytes 28
  10.3 34.3 %all-to-all-start = ((bf16[16,2,16,576]{3,2,1,0:T(8,128)(2,1)}), bf16[16,2,16,576]{3,2,1,0:T(8,128)(2,1)S(1)}, u32[]{:S(2)}, u32[]{:S(2)}) async-start(bf16[16,2,16,576]{3,2,1,0:T(8,128)(2,1)} %bitcast.3), calls=%async_computation | async-start | bytes 1310720 | tf_op jit(solution)/shard_map/all_to_all | solution.py:198
  16.7 13.3 %collective-permute-start.5 = (bf16[16,3712]{1,0:T(8,128)(2,1)S(1)}, bf16[16,3712]{1,0:T(8,128)(2,1)S(1)}, u32[]{:S(2)}, u32[]{:S(2)}) collective-permute-start(bf16[16,3712]{1,0:T(8,128)(2,1)S(1)} %reshape.113), channel_id=1, source_target_pairs={{0,5},{1,4},{2,7},{3,6},{4,1},{5,0},{6,3},{7,2},{8,13},{9,12},{10,... | collective-permute-start | bytes 356360 | tf_op jit(solution)/shard_map/ppermute | solution.py:32
  19.6 10.4 %collective-permute-start.4 = (bf16[16,3712]{1,0:T(8,128)(2,1)S(1)}, bf16[16,3712]{1,0:T(8,128)(2,1)S(1)}, u32[]{:S(2)}, u32[]{:S(2)}) collective-permute-start(bf16[16,3712]{1,0:T(8,128)(2,1)S(1)} %reshape.113), channel_id=1, source_target_pairs={{0,4},{1,5},{2,6},{3,7},{4,0},{5,1},{6,2},{7,3},{8,12},{9,13},{10,... | collective-permute-start | bytes 356360 | tf_op jit(solution)/shard_map/ppermute | solution.py:32
  19.7 6.5 %collective-permute-start.3 = (bf16[16,3712]{1,0:T(8,128)(2,1)S(1)}, bf16[16,3712]{1,0:T(8,128)(2,1)S(1)}, u32[]{:S(2)}, u32[]{:S(2)}) collective-permute-start(bf16[16,3712]{1,0:T(8,128)(2,1)S(1)} %reshape.113), channel_id=1, source_target_pairs={{0,1},{1,0},{2,3},{3,2},{4,5},{5,4},{6,7},{7,6},{8,9},{9,8},{10,11... | collective-permute-start | bytes 356360 | tf_op jit(solution)/shard_map/ppermute | solution.py:32
  30.0 1.9 %collective-permute-start.6 = (bf16[64,3712]{1,0:T(8,128)(2,1)S(1)}, bf16[64,3712]{1,0:T(8,128)(2,1)S(1)}, u32[]{:S(2)}, u32[]{:S(2)}) collective-permute-start(bf16[64,3712]{1,0:T(8,128)(2,1)S(1)} %constant_dynamic-update-slice_fusion.own_ref), channel_id=1, source_target_pairs={{0,2},{1,3},{2,0},{3,1},{4,6},{5,7},{6,4},{7,5},{8,10},{9,11},{10,... | collective-permute-start | bytes 1425416 | tf_op jit(solution)/shard_map/ppermute | solution.py:32
  39.0 1.9 %collective-permute-start.7 = (bf16[64,3584]{1,0:T(8,128)(2,1)S(1)}, bf16[64,3584]{1,0:T(8,128)(2,1)S(1)}, u32[]{:S(2)}, u32[]{:S(2)}) collective-permute-start(bf16[64,3584]{1,0:T(8,128)(2,1)S(1)} %get-tuple-element.5), channel_id=1, source_target_pairs={{0,2},{1,3},{2,0},{3,1},{4,6},{5,7},{6,4},{7,5},{8,10},{9,11},{10,... | collective-permute-start | bytes 1376264 | tf_op jit(solution)/shard_map/ppermute | solution.py:32
  40.8 4.4 %copy-start.4 = (bf16[1,2,4,576]{3,2,1,0:T(4,128)(2,1)S(1)}, bf16[1,2,4,576]{3,2,1,0:T(4,128)(2,1)}, u32[]{:S(2)}) copy-start(bf16[1,2,4,576]{3,2,1,0:T(4,128)(2,1)} %param.16) | copy-start | bytes 27652
  41.0 7.6 %collective-permute-start.8 = (bf16[16,3584]{1,0:T(8,128)(2,1)S(1)}, bf16[16,3584]{1,0:T(8,128)(2,1)S(1)}, u32[]{:S(2)}, u32[]{:S(2)}) collective-permute-start(bf16[16,3584]{1,0:T(8,128)(2,1)S(1)} %get-tuple-element.8), channel_id=1, source_target_pairs={{0,1},{1,0},{2,3},{3,2},{4,5},{5,4},{6,7},{7,6},{8,9},{9,8},{10,11... | collective-permute-start | bytes 344072 | tf_op jit(solution)/shard_map/ppermute | solution.py:32
  42.5 7.2 %collective-permute-start.10 = (bf16[16,3584]{1,0:T(8,128)(2,1)S(1)}, bf16[16,3584]{1,0:T(8,128)(2,1)S(1)}, u32[]{:S(2)}, u32[]{:S(2)}) collective-permute-start(bf16[16,3584]{1,0:T(8,128)(2,1)S(1)} %get-tuple-element.9), channel_id=1, source_target_pairs={{0,5},{1,4},{2,7},{3,6},{4,1},{5,0},{6,3},{7,2},{8,13},{9,12},{10,... | collective-permute-start | bytes 344072 | tf_op jit(solution)/shard_map/ppermute | solution.py:32
  44.0 7.1 %collective-permute-start.9 = (bf16[16,3584]{1,0:T(8,128)(2,1)S(1)}, bf16[16,3584]{1,0:T(8,128)(2,1)S(1)}, u32[]{:S(2)}, u32[]{:S(2)}) collective-permute-start(bf16[16,3584]{1,0:T(8,128)(2,1)S(1)} %get-tuple-element.10), channel_id=1, source_target_pairs={{0,4},{1,5},{2,6},{3,7},{4,0},{5,1},{6,2},{7,3},{8,12},{9,13},{10,... | collective-permute-start | bytes 344072 | tf_op jit(solution)/shard_map/ppermute | solution.py:32
  45.2 2.6 %copy-start.3 = (bf16[1,2,4,64,576]{4,3,2,1,0:T(8,128)(2,1)S(1)}, bf16[1,2,4,64,576]{4,3,2,1,0:T(8,128)(2,1)}, u32[]{:S(2)}) copy-start(bf16[1,2,4,64,576]{4,3,2,1,0:T(8,128)(2,1)} %param.17) | copy-start | bytes 1769476
  51.2 7.2 %collective-permute-start.11 = (bf16[4,3584]{1,0:T(4,128)(2,1)S(1)}, bf16[4,3584]{1,0:T(4,128)(2,1)S(1)}, u32[]{:S(2)}, u32[]{:S(2)}) collective-permute-start(bf16[4,3584]{1,0:T(4,128)(2,1)S(1)} %get-tuple-element.11), channel_id=1, source_target_pairs={{0,8},{1,9},{2,10},{3,11},{4,12},{5,13},{6,14},{7,15},{8,0},{9,1},... | collective-permute-start | bytes 86024 | tf_op jit(solution)/shard_map/ppermute | solution.py:32
  52.4 6.0 %collective-permute-start.13 = (bf16[4,3584]{1,0:T(4,128)(2,1)S(1)}, bf16[4,3584]{1,0:T(4,128)(2,1)S(1)}, u32[]{:S(2)}, u32[]{:S(2)}) collective-permute-start(bf16[4,3584]{1,0:T(4,128)(2,1)S(1)} %get-tuple-element.12), channel_id=1, source_target_pairs={{0,24},{1,25},{2,26},{3,27},{4,28},{5,29},{6,30},{7,31},{8,16},{9,... | collective-permute-start | bytes 86024 | tf_op jit(solution)/shard_map/ppermute | solution.py:32
  54.8 4.8 %collective-permute-start.12 = (bf16[4,3584]{1,0:T(4,128)(2,1)S(1)}, bf16[4,3584]{1,0:T(4,128)(2,1)S(1)}, u32[]{:S(2)}, u32[]{:S(2)}) collective-permute-start(bf16[4,3584]{1,0:T(4,128)(2,1)S(1)} %get-tuple-element.13), channel_id=1, source_target_pairs={{0,16},{1,17},{2,18},{3,19},{4,20},{5,21},{6,22},{7,23},{8,24},{9,... | collective-permute-start | bytes 86024 | tf_op jit(solution)/shard_map/ppermute | solution.py:32

commit v3 on v1

--- a/solution.py
+++ b/solution.py
@@ -218,33 +218,31 @@
     packed = jnp.concatenate([moe_rows[0], jnp.pad(extra, ((0, 0), (0, pad)))], axis=1)
     blocks = lax.axis_size(("section", "tp"))
     far, near, last = levels_of(peers, blocks)
-    low = blocks.bit_length() - 1
-    middle = near[low:]
-    ends = [1 << len(far), 1 << len(middle), 1 << len(last)]
-    moving = sent_pages.reshape(ends + [-1, width_lat])
-    for bit in middle:
-        moving = jnp.stack([moving[:, 0], exchange(moving[:, 1], 1 << bit)], axis=1)
+    middle = near[-1]
+    masks = masks_of(far)
     pooled = packed[None]
     for bits in pairs_of(far):
         pooled = jnp.concatenate([pooled] + [exchange(pooled, mask) for mask in masks_of(bits)[1:]], axis=0)
-    pooled, moving = lax.optimization_barrier((pooled, moving))
+    pooled, moving = lax.optimization_barrier((pooled, sent_pages))
+    moving = moving.reshape(len(masks), 2, 2, -1, width_lat)
     pooled = pooled.reshape(-1, packed.shape[1])
-    masks = masks_of(far)
     early = [exchange(moving[turn], masks[turn]) for turn in range(1, len(masks) - 1)]
     pooled = jnp.concatenate([pooled] + [exchange(pooled, mask) for mask in masks_of(near)[1:]], axis=0)
     pooled, early, moving = lax.optimization_barrier((pooled, early, moving))
-    late = [exchange(moving[turn], masks[turn]) for turn in range(max(1, len(masks) - 1), len(masks))]
+    crossed = exchange(jnp.stack([moving[0, 1]] + [part[1] for part in early]), 1 << middle)
+    late = [exchange(moving[-1, 0], masks[-1]), exchange(moving[-1, 1], masks[-1] | 1 << middle)]
     other = masks_of(last)[-1]
     first = me * owned
     kept, sent = experts_of(
         pooled, exchange(pooled, other), first, experts, expert_gate, expert_up, expert_down
     )
-    kept, sent, late = lax.optimization_barrier((kept, sent, late))
+    kept, sent, crossed, late = lax.optimization_barrier((kept, sent, crossed, late))
     mixed = kept.astype(jnp.float32) + exchange(sent, other).astype(jnp.float32)
-    mixed, late = lax.optimization_barrier((mixed.astype(jnp.bfloat16), late))
-    moving = jnp.stack([moving[0]] + list(early) + list(late), axis=0)
-    for bit in last:
-        moving = jnp.stack([moving[:, :, 0], exchange(moving[:, :, 1], 1 << bit)], axis=2)
+    mixed, crossed, late = lax.optimization_barrier((mixed.astype(jnp.bfloat16), crossed, late))
+    straight = jnp.stack([moving[0, 0]] + [part[0] for part in early] + [late[0]])
+    crossed = jnp.concatenate([crossed, late[1][None]])
+    away = exchange(jnp.stack([straight[:, 1], crossed[:, 1]], axis=1), other)
+    moving = jnp.stack([jnp.stack([straight[:, 0], crossed[:, 0]], axis=1), away], axis=2)
     mixed = collect(mixed, near)
     mixed, moving = lax.optimization_barrier((mixed, moving))
     for bits in pairs_of(far)[::-1]:

time: 66.7 us -> 63.8 us (0.957)
  waiting for transfers between devices: 21.5 us -> 16.6 us
  other arithmetic: 3.18 us -> 4.5 us
    ppermute x19 -> x20, waiting for transfers between devices: 21.5 us -> 16.6 us  [exchange(): return lax.ppermute(value, RANK, [(at, at ^ mask) for at in range(count)])]
    unnamed x9 -> x6, local copies, waits for them, and re-layouts: 1.16 us -> 0.02 us
    slice x2 -> x3, local copies, waits for them, and re-layouts: 0.09 us -> 1.08 us  [the longest x1 1.02 us: body(): moving[turn]]
    select_n x1, other arithmetic: 0.01 us -> 0.69 us  [body(): cache = arrived[slots].reshape(requests, most_pages * page_len, width_lat)]
    ppermute x19 -> x20, starting transfers between devices: 25.7 us -> 26.2 us  [exchange(): return lax.ppermute(value, RANK, [(at, at ^ mask) for at in range(count)])]
  transfers between devices with their start and end apart: 19 -> 20, of which waited for: 10 -> 8; matrix products, arithmetic and copies ran while one was open for 6% -> 8% of each run, Pallas kernels for 15% -> 16%
where the time goes in v3:
time: 63.8 us; the launch traced here: 63.4 us
  starting transfers between devices  26.2 us (41%)
  waiting for transfers between devices  16.6 us (26%)
  Pallas kernels  10 us (16%)
  other arithmetic  4.5 us (7%)
  matrix products  3.24 us (5%)
  local copies, waits for them, and re-layouts  1.98 us (3%)
  between operations  0.91 us (1%)
    ppermute x20, starting transfers between devices, exchange(): return lax.ppermute(value, RANK, [(at, at ^ mask) for at in range(count)])  26.2 us
    ppermute x20, waiting for transfers between devices, exchange(): return lax.ppermute(value, RANK, [(at, at ^ mask) for at in range(count)])  16.6 us
    pallas_call x1, Pallas kernels, experts_of(): pl.pallas_call(experts_kernel, out_shape=(half, half), in_specs=[pl.Block...  7.02 us
    pallas_call x1, Pallas kernels, pick_pages(): pl.pallas_call(functools.partial(pick_kernel, capp), out_shape=jax.ShapeD...  3.01 us
    dot_general x1, matrix products, attend(): jnp.einsum('rshk,rkv->rshv', weights, values, preferred_element_type=jnp....  1.94 us
  transfers between devices with their start and end apart: 20, of which 8 were waited for; matrix products, arithmetic and copies ran while one was open for 8% of the time, Pallas kernels for 16%

profile of v3, /device:TPU:0, one launch (start us, length us, event | category | flops | bytes accessed | tf_op | source)
XLA Modules:
  0.0 63.4 jit_solution(16097625184065734749)
XLA Ops:
  0.6 0.8 %select_reduce_fusion = f32[4,16]{1,0:T(4,128)S(1)} fusion(f32[4,8]{1,0:T(4,128)} %bitcast.106, s32[4,8]{1,0:T(4,128)} %bitcast.107), kind=kLoop, calls=%fused_computation.42 | loop fusion | flops 1472 | bytes 512 | tf_op jit(solution)/shard_map/reduce_sum | solution.py:213
  1.6 0.8 %maximum_bitcast_fusion.1 = bf16[1,4,3712]{2,1,0:T(4,128)(2,1)S(1)} fusion(bf16[4,128]{1,0:T(4,128)(2,1)S(1)} %fusion.30, bf16[4,3584]{1,0:T(4,128)(2,1)} %bitcast.105), kind=kLoop, calls=%fused_computation.40 | loop fusion | flops 59392 | bytes 59392 | tf_op jit(solution)/shard_map/broadcast_in_dim | solution.py:223
  2.4 3.1 %collective-permute-start = (bf16[1,4,3712]{2,1,0:T(4,128)(2,1)S(1)}, bf16[1,4,3712]{2,1,0:T(4,128)(2,1)S(1)}, u32[]{:S(2)}, u32[]{:S(2)}) collective-permute-start(bf16[1,4,3712]{2,1,0:T(4,128)(2,1)S(1)} %maximum_bitcast_fusion.1), channel_id=1, source_target_pairs={{0,8},{1,9},{2,10},{3,11},{4,12},{5,13},{6,14},{7,15},{8,0},{9,1},... | collective-permute-start | bytes 89096 | tf_op jit(solution)/shard_map/ppermute | solution.py:33
  5.4 2.6 %collective-permute-start.1 = (bf16[1,4,3712]{2,1,0:T(4,128)(2,1)S(1)}, bf16[1,4,3712]{2,1,0:T(4,128)(2,1)S(1)}, u32[]{:S(2)}, u32[]{:S(2)}) collective-permute-start(bf16[1,4,3712]{2,1,0:T(4,128)(2,1)S(1)} %maximum_bitcast_fusion.1), channel_id=1, source_target_pairs={{0,16},{1,17},{2,18},{3,19},{4,20},{5,21},{6,22},{7,23},{8,24},{9,... | collective-permute-start | bytes 89096 | tf_op jit(solution)/shard_map/ppermute | solution.py:33
  8.0 0.7 %compare_select_fusion = s32[2,16,1]{1,0,2:T(2,128)S(1)} fusion(s32[1,2,16]{2,1,0:T(2,128)} %param.14, s32[]{:T(128)} %axis_index.15), kind=kLoop, calls=%fused_computation.48 | loop fusion | flops 608 | bytes 260 | tf_op jit(solution)/shard_map/select_n | solution.py:256
  8.8 0.7 %iota_compare_fusion.3 = pred[2,260]{1,0:T(4,128)(4,1)S(1)} fusion(s32[2]{0:T(128)} %bitcast.109), kind=kLoop, calls=%fused_computation.49 | loop fusion | flops 520 | bytes 528 | tf_op jit(solution)/shard_map/lt | solution.py:174
  9.6 3.0 %pick.1 = bf16[32,16,576]{2,1,0:T(8,128)(2,1)} custom-call(s32[1]{0:T(128)} %bitcast.1.me_ref, s32[32]{0:T(128)} %bitcast.108, bf16[32,16,576]{2,1,0:T(8,128)(2,1)} %bitcast.95), custom_call_target="tpu_custom_call" | custom-call | bytes 1179648 | tf_op jit(solution)/shard_map/pick/pallas_call | solution.py:156
  12.7 1.0 %collective-permute-done.2 = bf16[1,4,3712]{2,1,0:T(4,128)(2,1)S(1)} collective-permute-done((bf16[1,4,3712]{2,1,0:T(4,128)(2,1)S(1)}, bf16[1,4,3712]{2,1,0:T(4,128)(2,1)S(1)}, u32[]{:S(2)}, u32[]{:S(2)}) %collective-permute-start.2) | collective-permute-done | bytes 29728 | tf_op jit(solution)/shard_map/ppermute | solution.py:33
  13.9 1.6 %collective-permute-start.3 = (bf16[16,3712]{1,0:T(8,128)(2,1)S(1)}, bf16[16,3712]{1,0:T(8,128)(2,1)S(1)}, u32[]{:S(2)}, u32[]{:S(2)}) collective-permute-start(bf16[16,3712]{1,0:T(8,128)(2,1)S(1)} %reshape.166), channel_id=1, source_target_pairs={{0,1},{1,0},{2,3},{3,2},{4,5},{5,4},{6,7},{7,6},{8,9},{9,8},{10,11... | collective-permute-start | bytes 356360 | tf_op jit(solution)/shard_map/ppermute | solution.py:33
  15.4 1.5 %collective-permute-start.4 = (bf16[16,3712]{1,0:T(8,128)(2,1)S(1)}, bf16[16,3712]{1,0:T(8,128)(2,1)S(1)}, u32[]{:S(2)}, u32[]{:S(2)}) collective-permute-start(bf16[16,3712]{1,0:T(8,128)(2,1)S(1)} %reshape.166), channel_id=1, source_target_pairs={{0,4},{1,5},{2,6},{3,7},{4,0},{5,1},{6,2},{7,3},{8,12},{9,13},{10,... | collective-permute-start | bytes 356360 | tf_op jit(solution)/shard_map/ppermute | solution.py:33
  17.4 1.0 %fusion.38 = (bf16[8,16,576]{2,1,0:T(8,128)(2,1)S(1)}, bf16[8,16,576]{2,1,0:T(8,128)(2,1)S(1)}) fusion(bf16[32,16,576]{2,1,0:T(8,128)(2,1)} %pick.1), kind=kLoop, calls=%fused_computation.70 | loop fusion | bytes 589824 | tf_op jit(solution)/shard_map/slice | solution.py:229
  18.5 3.3 %collective-permute-start.7 = (bf16[2,2,32,576]{3,2,1,0:T(8,128)(2,1)S(1)}, bf16[2,2,32,576]{3,2,1,0:T(8,128)(2,1)S(1)}, u32[]{:S(2)}, u32[]{:S(2)}) collective-permute-start(bf16[2,2,32,576]{3,2,1,0:T(8,128)(2,1)S(1)} %bitcast.102), channel_id=1, source_target_pairs={{0,16},{1,17},{2,18},{3,19},{4,20},{5,21},{6,22},{7,23},{8,24},{9,... | collective-permute-start | bytes 442376 | tf_op jit(solution)/shard_map/ppermute | solution.py:33
  21.8 0.9 %collective-permute-done.5 = bf16[16,3712]{1,0:T(8,128)(2,1)S(1)} collective-permute-done((bf16[16,3712]{1,0:T(8,128)(2,1)S(1)}, bf16[16,3712]{1,0:T(8,128)(2,1)S(1)}, u32[]{:S(2)}, u32[]{:S(2)}) %collective-permute-start.5) | collective-permute-done | bytes 118816 | tf_op jit(solution)/shard_map/ppermute | solution.py:33
  22.7 1.9 %collective-permute-done.6 = bf16[2,2,32,576]{3,2,1,0:T(8,128)(2,1)S(1)} collective-permute-done((bf16[2,2,32,576]{3,2,1,0:T(8,128)(2,1)S(1)}, bf16[2,2,32,576]{3,2,1,0:T(8,128)(2,1)S(1)}, u32[]{:S(2)}, u32[]{:S(2)}) %collective-permute-start.6) | collective-permute-done | bytes 147488 | tf_op jit(solution)/shard_map/ppermute | solution.py:33
  24.6 2.9 %collective-permute-done.7 = bf16[2,2,32,576]{3,2,1,0:T(8,128)(2,1)S(1)} collective-permute-done((bf16[2,2,32,576]{3,2,1,0:T(8,128)(2,1)S(1)}, bf16[2,2,32,576]{3,2,1,0:T(8,128)(2,1)S(1)}, u32[]{:S(2)}, u32[]{:S(2)}) %collective-permute-start.7) | collective-permute-done | bytes 147488 | tf_op jit(solution)/shard_map/ppermute | solution.py:33
  27.6 1.7 %collective-permute-start.9 = (bf16[3,2,32,576]{3,2,1,0:T(8,128)(2,1)S(1)}, bf16[3,2,32,576]{3,2,1,0:T(8,128)(2,1)S(1)}, u32[]{:S(2)}, u32[]{:S(2)}) collective-permute-start(bf16[3,2,32,576]{3,2,1,0:T(8,128)(2,1)S(1)} %pad_maximum_fusion.4), channel_id=1, source_target_pairs={{0,4},{1,5},{2,6},{3,7},{4,0},{5,1},{6,2},{7,3},{8,12},{9,13},{10,... | collective-permute-start | bytes 663560 | tf_op jit(solution)/shard_map/ppermute | solution.py:33
  29.3 2.6 %collective-permute-start.10 = (bf16[2,32,576]{2,1,0:T(8,128)(2,1)S(1)}, bf16[2,32,576]{2,1,0:T(8,128)(2,1)S(1)}, u32[]{:S(2)}, u32[]{:S(2)}) collective-permute-start(bf16[2,32,576]{2,1,0:T(8,128)(2,1)S(1)} %get-tuple-element.44), channel_id=1, source_target_pairs={{0,24},{1,25},{2,26},{3,27},{4,28},{5,29},{6,30},{7,31},{8,16},{9,... | collective-permute-start | bytes 221192 | tf_op jit(solution)/shard_map/ppermute | solution.py:33
  32.0 1.0 %collective-permute-start.11 = (bf16[2,32,576]{2,1,0:T(8,128)(2,1)S(1)}, bf16[2,32,576]{2,1,0:T(8,128)(2,1)S(1)}, u32[]{:S(2)}, u32[]{:S(2)}) collective-permute-start(bf16[2,32,576]{2,1,0:T(8,128)(2,1)S(1)} %get-tuple-element.43), channel_id=1, source_target_pairs={{0,28},{1,29},{2,30},{3,31},{4,24},{5,25},{6,26},{7,27},{8,20},{9,... | collective-permute-start | bytes 221192 | tf_op jit(solution)/shard_map/ppermute | solution.py:33
  32.9 7.0 %experts.1 = (bf16[64,3584]{1,0:T(8,128)(2,1)S(1)}, bf16[64,3584]{1,0:T(8,128)(2,1)S(1)}) custom-call(s32[2]{0:T(128)S(1)} %pad_add_fusion.first_ref, bf16[64,3712]{1,0:T(8,128)(2,1)S(1)} %pad_maximum_fusion.2.own_ref, bf16[64,3712]{1,0:T(8,128)(2,1)S(1)} %collective-permute-done.8.got_ref, bf16[1,3584,512]{2,1,0:T(8,128)(2,1)} %gate_hbm.1, ...), custom_call_target="tpu_custom_call" | custom-call | flops 5637144576 | bytes 11010048 | tf_op jit(solution)/shard_map/experts/pallas_call | solution.py:118
  40.1 1.8 %collective-permute-done.12 = bf16[64,3584]{1,0:T(8,128)(2,1)S(1)} collective-permute-done((bf16[64,3584]{1,0:T(8,128)(2,1)S(1)}, bf16[64,3584]{1,0:T(8,128)(2,1)S(1)}, u32[]{:S(2)}, u32[]{:S(2)}) %collective-permute-start.12) | collective-permute-done | bytes 458784 | tf_op jit(solution)/shard_map/ppermute | solution.py:33
  42.4 1.7 %collective-permute-start.13 = (bf16[16,3584]{1,0:T(8,128)(2,1)S(1)}, bf16[16,3584]{1,0:T(8,128)(2,1)S(1)}, u32[]{:S(2)}, u32[]{:S(2)}) collective-permute-start(bf16[16,3584]{1,0:T(8,128)(2,1)S(1)} %get-tuple-element.48), channel_id=1, source_target_pairs={{0,1},{1,0},{2,3},{3,2},{4,5},{5,4},{6,7},{7,6},{8,9},{9,8},{10,11... | collective-permute-start | bytes 344072 | tf_op jit(solution)/shard_map/ppermute | solution.py:33
  44.1 1.5 %collective-permute-start.14 = (bf16[16,3584]{1,0:T(8,128)(2,1)S(1)}, bf16[16,3584]{1,0:T(8,128)(2,1)S(1)}, u32[]{:S(2)}, u32[]{:S(2)}) collective-permute-start(bf16[16,3584]{1,0:T(8,128)(2,1)S(1)} %get-tuple-element.50), channel_id=1, source_target_pairs={{0,4},{1,5},{2,6},{3,7},{4,0},{5,1},{6,2},{7,3},{8,12},{9,13},{10,... | collective-permute-start | bytes 344072 | tf_op jit(solution)/shard_map/ppermute | solution.py:33
  46.0 1.9 %collective-permute-done.13 = bf16[16,3584]{1,0:T(8,128)(2,1)S(1)} collective-permute-done((bf16[16,3584]{1,0:T(8,128)(2,1)S(1)}, bf16[16,3584]{1,0:T(8,128)(2,1)S(1)}, u32[]{:S(2)}, u32[]{:S(2)}) %collective-permute-start.13) | collective-permute-done | bytes 114720 | tf_op jit(solution)/shard_map/ppermute | solution.py:33
  47.9 3.8 %collective-permute-done.14 = bf16[16,3584]{1,0:T(8,128)(2,1)S(1)} collective-permute-done((bf16[16,3584]{1,0:T(8,128)(2,1)S(1)}, bf16[16,3584]{1,0:T(8,128)(2,1)S(1)}, u32[]{:S(2)}, u32[]{:S(2)}) %collective-permute-start.14) | collective-permute-done | bytes 114720 | tf_op jit(solution)/shard_map/ppermute | solution.py:33
  51.9 0.7 %gather_fusion = bf16[32,16,576]{2,1,0:T(8,128)(2,1)S(1)} fusion(bf16[32,16,576]{2,1,0:T(8,128)(2,1)S(1)} %bitcast.94, s32[1024]{0:T(1024)S(1)} %pad_clamp_fusion), kind=kCustom, calls=%fused_computation | custom fusion | bytes 1179776 | tf_op jit(solution)/shard_map/gather | solution.py:256
  52.5 0.6 fusion.4
  53.1 0.7 %fusion.44 = f32[2,4,64]{2,1,0:T(4,128)S(1)} fusion(bf16[2,4,576]{2,1,0:T(4,128)(2,1)S(1)} %bitcast.111, bf16[1,2,4,64,576]{4,3,2,1,0:T(8,128)(2,1)S(1)} %copy-done, bf16[2,256,576]{2,1,0:T(8,128)(2,1)S(1)} %bitcast.97, pred[2,4,260]{2,1,0:T(4,128)(4,1)S(1)} %broadcast_or_fusion), kind=kOutput, calls=%fused_computation.76 | convolution fusion | flops 155085056 | bytes 1192992 | tf_op jit(solution)/shard_map/sub | solution.py:179
  54.0 3.1 %collective-permute-start.18 = (bf16[4,3584]{1,0:T(4,128)(2,1)S(1)}, bf16[4,3584]{1,0:T(4,128)(2,1)S(1)}, u32[]{:S(2)}, u32[]{:S(2)}) collective-permute-start(bf16[4,3584]{1,0:T(4,128)(2,1)S(1)} %get-tuple-element.59), channel_id=1, source_target_pairs={{0,16},{1,17},{2,18},{3,19},{4,20},{5,21},{6,22},{7,23},{8,24},{9,... | collective-permute-start | bytes 86024 | tf_op jit(solution)/shard_map/ppermute | solution.py:33
  57.1 1.2 %collective-permute-start.19 = (bf16[4,3584]{1,0:T(4,128)(2,1)S(1)}, bf16[4,3584]{1,0:T(4,128)(2,1)S(1)}, u32[]{:S(2)}, u32[]{:S(2)}) collective-permute-start(bf16[4,3584]{1,0:T(4,128)(2,1)S(1)} %get-tuple-element.58), channel_id=1, source_target_pairs={{0,24},{1,25},{2,26},{3,27},{4,28},{5,29},{6,30},{7,31},{8,16},{9,... | collective-permute-start | bytes 86024 | tf_op jit(solution)/shard_map/ppermute | solution.py:33
  58.4 1.9 %fusion.5 = bf16[1,2,4,64,512]{4,3,2,1,0:T(8,128)(2,1)} fusion(bf16[2,256,576]{2,1,0:T(8,128)(2,1)S(1)} %bitcast.98, bf16[2,4,576]{2,1,0:T(4,128)(2,1)S(1)} %bitcast.112, f32[2,4,64]{2,1,0:T(4,128)S(1)} %fusion.44, f32[2,4,64,260]{3,2,1,0:T(8,128)S(1)} %fusion.4), kind=kOutput, calls=%fused_computation.8 | convolution fusion | flops 138042112 | bytes 2766848 | tf_op jit(solution)/shard_map/rshk,rkv->rshv/dot_general | solution.py:182
  60.3 2.5 %collective-permute-done.19 = bf16[4,3584]{1,0:T(4,128)(2,1)S(1)} collective-permute-done((bf16[4,3584]{1,0:T(4,128)(2,1)S(1)}, bf16[4,3584]{1,0:T(4,128)(2,1)S(1)}, u32[]{:S(2)}, u32[]{:S(2)}) %collective-permute-start.19) | collective-permute-done | bytes 28704 | tf_op jit(solution)/shard_map/ppermute | solution.py:33
  62.8 0.6 %fusion.19 = bf16[1,4,3584]{2,1,0:T(4,128)(2,1)} fusion(bf16[4,3584]{1,0:T(4,128)(2,1)S(1)} %collective-permute-done.19, bf16[4,3584]{1,0:T(4,128)(2,1)S(1)} %collective-permute-done.18, bf16[4,3584]{1,0:T(4,128)(2,1)S(1)} %collective-permute-done.17, bf16[16,3584]{1,0:T(8,128)(2,1)S(1)} %add_convert_fusion.1), kind=kLoop, calls=%fused_computation.41 | loop fusion | flops 114688 | bytes 143360 | tf_op jit(solution)/shard_map/broadcast_in_dim | solution.py:258
  (51 shorter events, 2.4 us)
Async XLA Ops:
  0.6 51.9 %copy-start = (bf16[1,2,4,64,576]{4,3,2,1,0:T(8,128)(2,1)S(1)}, bf16[1,2,4,64,576]{4,3,2,1,0:T(8,128)(2,1)}, u32[]{:S(2)}) copy-start(bf16[1,2,4,64,576]{4,3,2,1,0:T(8,128)(2,1)} %param.17) | copy-start | bytes 1769476
  2.4 10.3 %collective-permute-start = (bf16[1,4,3712]{2,1,0:T(4,128)(2,1)S(1)}, bf16[1,4,3712]{2,1,0:T(4,128)(2,1)S(1)}, u32[]{:S(2)}, u32[]{:S(2)}) collective-permute-start(bf16[1,4,3712]{2,1,0:T(4,128)(2,1)S(1)} %maximum_bitcast_fusion.1), channel_id=1, source_target_pairs={{0,8},{1,9},{2,10},{3,11},{4,12},{5,13},{6,14},{7,15},{8,0},{9,1},... | collective-permute-start | bytes 89096 | tf_op jit(solution)/shard_map/ppermute | solution.py:33
  5.4 7.2 %collective-permute-start.1 = (bf16[1,4,3712]{2,1,0:T(4,128)(2,1)S(1)}, bf16[1,4,3712]{2,1,0:T(4,128)(2,1)S(1)}, u32[]{:S(2)}, u32[]{:S(2)}) collective-permute-start(bf16[1,4,3712]{2,1,0:T(4,128)(2,1)S(1)} %maximum_bitcast_fusion.1), channel_id=1, source_target_pairs={{0,16},{1,17},{2,18},{3,19},{4,20},{5,21},{6,22},{7,23},{8,24},{9,... | collective-permute-start | bytes 89096 | tf_op jit(solution)/shard_map/ppermute | solution.py:33
  8.0 5.7 %collective-permute-start.2 = (bf16[1,4,3712]{2,1,0:T(4,128)(2,1)S(1)}, bf16[1,4,3712]{2,1,0:T(4,128)(2,1)S(1)}, u32[]{:S(2)}, u32[]{:S(2)}) collective-permute-start(bf16[1,4,3712]{2,1,0:T(4,128)(2,1)S(1)} %maximum_bitcast_fusion.1), channel_id=1, source_target_pairs={{0,24},{1,25},{2,26},{3,27},{4,28},{5,29},{6,30},{7,31},{8,16},{9,... | collective-permute-start | bytes 89096 | tf_op jit(solution)/shard_map/ppermute | solution.py:33
  12.6 14.8 %copy-start.1 = (bf16[32,16,576]{2,1,0:T(8,128)(2,1)S(1)}, bf16[32,16,576]{2,1,0:T(8,128)(2,1)}, u32[]{:S(2)}) copy-start(bf16[32,16,576]{2,1,0:T(8,128)(2,1)} %pick.1) | copy-start | bytes 1769476
  13.9 7.9 %collective-permute-start.3 = (bf16[16,3712]{1,0:T(8,128)(2,1)S(1)}, bf16[16,3712]{1,0:T(8,128)(2,1)S(1)}, u32[]{:S(2)}, u32[]{:S(2)}) collective-permute-start(bf16[16,3712]{1,0:T(8,128)(2,1)S(1)} %reshape.166), channel_id=1, source_target_pairs={{0,1},{1,0},{2,3},{3,2},{4,5},{5,4},{6,7},{7,6},{8,9},{9,8},{10,11... | collective-permute-start | bytes 356360 | tf_op jit(solution)/shard_map/ppermute | solution.py:33
  15.4 6.4 %collective-permute-start.4 = (bf16[16,3712]{1,0:T(8,128)(2,1)S(1)}, bf16[16,3712]{1,0:T(8,128)(2,1)S(1)}, u32[]{:S(2)}, u32[]{:S(2)}) collective-permute-start(bf16[16,3712]{1,0:T(8,128)(2,1)S(1)} %reshape.166), channel_id=1, source_target_pairs={{0,4},{1,5},{2,6},{3,7},{4,0},{5,1},{6,2},{7,3},{8,12},{9,13},{10,... | collective-permute-start | bytes 356360 | tf_op jit(solution)/shard_map/ppermute | solution.py:33
  16.9 5.7 %collective-permute-start.5 = (bf16[16,3712]{1,0:T(8,128)(2,1)S(1)}, bf16[16,3712]{1,0:T(8,128)(2,1)S(1)}, u32[]{:S(2)}, u32[]{:S(2)}) collective-permute-start(bf16[16,3712]{1,0:T(8,128)(2,1)S(1)} %reshape.166), channel_id=1, source_target_pairs={{0,5},{1,4},{2,7},{3,6},{4,1},{5,0},{6,3},{7,2},{8,13},{9,12},{10,... | collective-permute-start | bytes 356360 | tf_op jit(solution)/shard_map/ppermute | solution.py:33
  18.4 6.1 %collective-permute-start.6 = (bf16[2,2,32,576]{3,2,1,0:T(8,128)(2,1)S(1)}, bf16[2,2,32,576]{3,2,1,0:T(8,128)(2,1)S(1)}, u32[]{:S(2)}, u32[]{:S(2)}) collective-permute-start(bf16[2,2,32,576]{3,2,1,0:T(8,128)(2,1)S(1)} %bitcast.103), channel_id=1, source_target_pairs={{0,8},{1,9},{2,10},{3,11},{4,12},{5,13},{6,14},{7,15},{8,0},{9,1},... | collective-permute-start | bytes 442376 | tf_op jit(solution)/shard_map/ppermute | solution.py:33
  18.5 8.9 %collective-permute-start.7 = (bf16[2,2,32,576]{3,2,1,0:T(8,128)(2,1)S(1)}, bf16[2,2,32,576]{3,2,1,0:T(8,128)(2,1)S(1)}, u32[]{:S(2)}, u32[]{:S(2)}) collective-permute-start(bf16[2,2,32,576]{3,2,1,0:T(8,128)(2,1)S(1)} %bitcast.102), channel_id=1, source_target_pairs={{0,16},{1,17},{2,18},{3,19},{4,20},{5,21},{6,22},{7,23},{8,24},{9,... | collective-permute-start | bytes 442376 | tf_op jit(solution)/shard_map/ppermute | solution.py:33
  27.4 5.5 %collective-permute-start.8 = (bf16[64,3712]{1,0:T(8,128)(2,1)S(1)}, bf16[64,3712]{1,0:T(8,128)(2,1)S(1)}, u32[]{:S(2)}, u32[]{:S(2)}) collective-permute-start(bf16[64,3712]{1,0:T(8,128)(2,1)S(1)} %pad_maximum_fusion.2.own_ref), channel_id=1, source_target_pairs={{0,2},{1,3},{2,0},{3,1},{4,6},{5,7},{6,4},{7,5},{8,10},{9,11},{10,... | collective-permute-start | bytes 1425416 | tf_op jit(solution)/shard_map/ppermute | solution.py:33
  27.6 12.4 %collective-permute-start.9 = (bf16[3,2,32,576]{3,2,1,0:T(8,128)(2,1)S(1)}, bf16[3,2,32,576]{3,2,1,0:T(8,128)(2,1)S(1)}, u32[]{:S(2)}, u32[]{:S(2)}) collective-permute-start(bf16[3,2,32,576]{3,2,1,0:T(8,128)(2,1)S(1)} %pad_maximum_fusion.4), channel_id=1, source_target_pairs={{0,4},{1,5},{2,6},{3,7},{4,0},{5,1},{6,2},{7,3},{8,12},{9,13},{10,... | collective-permute-start | bytes 663560 | tf_op jit(solution)/shard_map/ppermute | solution.py:33
  29.3 10.6 %collective-permute-start.10 = (bf16[2,32,576]{2,1,0:T(8,128)(2,1)S(1)}, bf16[2,32,576]{2,1,0:T(8,128)(2,1)S(1)}, u32[]{:S(2)}, u32[]{:S(2)}) collective-permute-start(bf16[2,32,576]{2,1,0:T(8,128)(2,1)S(1)} %get-tuple-element.44), channel_id=1, source_target_pairs={{0,24},{1,25},{2,26},{3,27},{4,28},{5,29},{6,30},{7,31},{8,16},{9,... | collective-permute-start | bytes 221192 | tf_op jit(solution)/shard_map/ppermute | solution.py:33
  32.0 8.0 %collective-permute-start.11 = (bf16[2,32,576]{2,1,0:T(8,128)(2,1)S(1)}, bf16[2,32,576]{2,1,0:T(8,128)(2,1)S(1)}, u32[]{:S(2)}, u32[]{:S(2)}) collective-permute-start(bf16[2,32,576]{2,1,0:T(8,128)(2,1)S(1)} %get-tuple-element.43), channel_id=1, source_target_pairs={{0,28},{1,29},{2,30},{3,31},{4,24},{5,25},{6,26},{7,27},{8,20},{9,... | collective-permute-start | bytes 221192 | tf_op jit(solution)/shard_map/ppermute | solution.py:33
  40.0 1.9 %collective-permute-start.12 = (bf16[64,3584]{1,0:T(8,128)(2,1)S(1)}, bf16[64,3584]{1,0:T(8,128)(2,1)S(1)}, u32[]{:S(2)}, u32[]{:S(2)}) collective-permute-start(bf16[64,3584]{1,0:T(8,128)(2,1)S(1)} %get-tuple-element.30), channel_id=1, source_target_pairs={{0,2},{1,3},{2,0},{3,1},{4,6},{5,7},{6,4},{7,5},{8,10},{9,11},{10,... | collective-permute-start | bytes 1376264 | tf_op jit(solution)/shard_map/ppermute | solution.py:33
  42.2 9.6 %collective-permute-start.16 = (bf16[4,2,32,576]{3,2,1,0:T(8,128)(2,1)S(1)}, bf16[4,2,32,576]{3,2,1,0:T(8,128)(2,1)S(1)}, u32[]{:S(2)}, u32[]{:S(2)}) collective-permute-start(bf16[4,2,32,576]{3,2,1,0:T(8,128)(2,1)S(1)} %fusion.17), channel_id=1, source_target_pairs={{0,2},{1,3},{2,0},{3,1},{4,6},{5,7},{6,4},{7,5},{8,10},{9,11},{10,... | collective-permute-start | bytes 884744 | tf_op jit(solution)/shard_map/ppermute | solution.py:33
  42.4 5.5 %collective-permute-start.13 = (bf16[16,3584]{1,0:T(8,128)(2,1)S(1)}, bf16[16,3584]{1,0:T(8,128)(2,1)S(1)}, u32[]{:S(2)}, u32[]{:S(2)}) collective-permute-start(bf16[16,3584]{1,0:T(8,128)(2,1)S(1)} %get-tuple-element.48), channel_id=1, source_target_pairs={{0,1},{1,0},{2,3},{3,2},{4,5},{5,4},{6,7},{7,6},{8,9},{9,8},{10,11... | collective-permute-start | bytes 344072 | tf_op jit(solution)/shard_map/ppermute | solution.py:33
  44.1 7.6 %collective-permute-start.14 = (bf16[16,3584]{1,0:T(8,128)(2,1)S(1)}, bf16[16,3584]{1,0:T(8,128)(2,1)S(1)}, u32[]{:S(2)}, u32[]{:S(2)}) collective-permute-start(bf16[16,3584]{1,0:T(8,128)(2,1)S(1)} %get-tuple-element.50), channel_id=1, source_target_pairs={{0,4},{1,5},{2,6},{3,7},{4,0},{5,1},{6,2},{7,3},{8,12},{9,13},{10,... | collective-permute-start | bytes 344072 | tf_op jit(solution)/shard_map/ppermute | solution.py:33
  45.6 6.1 %collective-permute-start.15 = (bf16[16,3584]{1,0:T(8,128)(2,1)S(1)}, bf16[16,3584]{1,0:T(8,128)(2,1)S(1)}, u32[]{:S(2)}, u32[]{:S(2)}) collective-permute-start(bf16[16,3584]{1,0:T(8,128)(2,1)S(1)} %get-tuple-element.49), channel_id=1, source_target_pairs={{0,5},{1,4},{2,7},{3,6},{4,1},{5,0},{6,3},{7,2},{8,13},{9,12},{10,... | collective-permute-start | bytes 344072 | tf_op jit(solution)/shard_map/ppermute | solution.py:33
  51.7 0.8 %copy-start.2 = (bf16[1,2,4,576]{3,2,1,0:T(4,128)(2,1)S(1)}, bf16[1,2,4,576]{3,2,1,0:T(4,128)(2,1)}, u32[]{:S(2)}) copy-start(bf16[1,2,4,576]{3,2,1,0:T(4,128)(2,1)} %param.16) | copy-start | bytes 27652
  53.9 6.4 %collective-permute-start.17 = (bf16[4,3584]{1,0:T(4,128)(2,1)S(1)}, bf16[4,3584]{1,0:T(4,128)(2,1)S(1)}, u32[]{:S(2)}, u32[]{:S(2)}) collective-permute-start(bf16[4,3584]{1,0:T(4,128)(2,1)S(1)} %get-tuple-element.57), channel_id=1, source_target_pairs={{0,8},{1,9},{2,10},{3,11},{4,12},{5,13},{6,14},{7,15},{8,0},{9,1},... | collective-permute-start | bytes 86024 | tf_op jit(solution)/shard_map/ppermute | solution.py:33
  54.0 6.3 %collective-permute-start.18 = (bf16[4,3584]{1,0:T(4,128)(2,1)S(1)}, bf16[4,3584]{1,0:T(4,128)(2,1)S(1)}, u32[]{:S(2)}, u32[]{:S(2)}) collective-permute-start(bf16[4,3584]{1,0:T(4,128)(2,1)S(1)} %get-tuple-element.59), channel_id=1, source_target_pairs={{0,16},{1,17},{2,18},{3,19},{4,20},{5,21},{6,22},{7,23},{8,24},{9,... | collective-permute-start | bytes 86024 | tf_op jit(solution)/shard_map/ppermute | solution.py:33
  57.1 5.7 %collective-permute-start.19 = (bf16[4,3584]{1,0:T(4,128)(2,1)S(1)}, bf16[4,3584]{1,0:T(4,128)(2,1)S(1)}, u32[]{:S(2)}, u32[]{:S(2)}) collective-permute-start(bf16[4,3584]{1,0:T(4,128)(2,1)S(1)} %get-tuple-element.58), channel_id=1, source_target_pairs={{0,24},{1,25},{2,26},{3,27},{4,28},{5,29},{6,30},{7,31},{8,16},{9,... | collective-permute-start | bytes 86024 | tf_op jit(solution)/shard_map/ppermute | solution.py:33
